TPU v7x, 128 devices: a whole 4x4x4 slice. The times are simulated.
128 devices in a mesh: dp: 32 (over z, y, core), mp: 4 (over x).
Axes of the slice: x: 4, y: 4, z: 4, core: 2. Of those that a mesh axis runs over, the one named last changes fastest.
Arguments:
- features: bfloat16 [262144, 512], P('dp', 'mp'), may hold values from -6 to 6
- conv6_weight: bfloat16 [1024, 512], P('dp', 'mp'), may hold values from -0.1875 to 0.1875
- conv7_weight: bfloat16 [1024, 512], P('dp', 'mp'), may hold values from -0.1875 to 0.1875
- frame_grads: bfloat16 [65536, 512], P('dp', 'mp'), may hold values from -0.29882812 to 0.29882812
- frame_dest: int32 [65536], replicated, may hold values from 0 to 65535, as said below
- lengths: int32 [128], P('dp'), may hold values from 41360 to 163920
Outputs:
- grad_features: bfloat16 [262144, 512], P('dp', 'mp')
- grad_conv6: float32 [1024, 512], P('dp', 'mp')
- grad_conv7: float32 [1024, 512], P('dp', 'mp')
Inputs may be any that keep to these rules, and one draw needn't show every extreme that they name: frame_dest maps the packed slots one to one onto all waveform frames; frame f belongs to the waveform owner f // 2048, slot j lies on transformer owner j // 2048. Every transformer owner sends at most 192 frames to one waveform owner and exactly 192 to one of them; every waveform owner receives exactly 192 frames from one transformer owner. `lengths`: entry d * 4 + u belongs to the utterance in output frames (d * 4 + u) * 512 onward.
All inputs are finite; a program needn't handle non-finite values.
Results may differ from a plain program's by a relative error of at most 0.006.
Values may be sent and summed in bfloat16 or wider, within the bound.
A program may use at most 128 MiB of HBM per device.

v0:
```python
import jax
import jax.numpy as jnp
from jax import lax
from jax.sharding import PartitionSpec as P

inv_root_two = 0.7071067811865476
inv_root_tau = 0.3989422804014327


def gelu_exact(values):
    return 0.5 * values * (1.0 + jax.scipy.special.erf(values * inv_root_two))


def gelu_slope(values):
    return (
        0.5 * (1.0 + jax.scipy.special.erf(values * inv_root_two))
        + values * jnp.exp(-0.5 * values * values) * inv_root_tau
    )


def reduce_kernel(left, right):
    return lax.psum_scatter(
        lax.dot_general(left, right, (((0,), (0,)), ((), ())), preferred_element_type=jnp.float32),
        "dp",
        scatter_dimension=0,
        tiled=True,
    )


def times_transpose(left, right):
    return lax.dot_general(
        left, right, (((1,), (1,)), ((), ())), preferred_element_type=jnp.float32
    )


def join_channels(values):
    return lax.all_gather(values, "mp", axis=1, tiled=True)


def spread_channels(values):
    return lax.psum_scatter(values, "mp", scatter_dimension=1, tiled=True)


def route_frames(frame_grads, frame_dest, lengths):
    dp_count = lax.axis_size("dp")
    own_index = lax.axis_index("dp")
    frames = frame_grads.shape[0]
    capacity = 3 * frames // dp_count
    own_slots = lax.dynamic_slice_in_dim(frame_dest, own_index * frames, frames, 0)
    own_dest = own_slots // frames
    own_rows = own_slots % frames
    owner_ids = jnp.arange(dp_count, dtype=jnp.int32)
    counts = jnp.sum((own_dest[:, None] == owner_ids[None, :]).astype(jnp.int32), axis=0)
    starts = jnp.cumsum(counts) - counts
    grouped = jnp.argsort(own_dest, stable=True)
    bucket_pos = jnp.arange(capacity, dtype=jnp.int32)[None, :]
    filled = bucket_pos < counts[:, None]
    pick_index = jnp.minimum(starts[:, None] + bucket_pos, frames - 1)
    source_row = grouped[pick_index]
    outbox = jnp.where(filled[:, :, None], frame_grads[source_row], jnp.zeros((), jnp.bfloat16))
    target_rows = jnp.where(filled, own_rows[source_row], frames)
    arrived, arrived_rows = (
        lax.all_to_all(outbox, "dp", split_axis=0, concat_axis=0, tiled=True),
        lax.all_to_all(target_rows, "dp", split_axis=0, concat_axis=0, tiled=True),
    )
    placing = jnp.argsort(arrived_rows.reshape(-1), stable=True)[:frames]
    routed = arrived.reshape(dp_count * capacity, arrived.shape[2])[placing]
    valid_len = (lengths - 400) // 320 + 1
    utter_len = frames // lengths.shape[0]
    positions = jnp.arange(frames, dtype=jnp.int32)
    limits = jnp.repeat(valid_len, utter_len, total_repeat_length=frames)
    live_mask = positions % utter_len < limits
    return jnp.where(live_mask[:, None], routed, jnp.zeros_like(routed))


def body(features, conv6_weight, conv7_weight, frame_grads, frame_dest, lengths):
    masked = route_frames(frame_grads, frame_dest, lengths)
    weight_six, weight_seven = (
        lax.all_gather(conv6_weight, "dp", axis=0, tiled=True),
        lax.all_gather(conv7_weight, "dp", axis=0, tiled=True),
    )
    frames = frame_grads.shape[0]
    full_width = weight_six.shape[0] // 2
    joined = join_channels(features)
    in_pairs = joined.reshape(joined.shape[0] // 2, 2 * joined.shape[1])
    pre_six = jnp.dot(in_pairs, weight_six, preferred_element_type=jnp.float32)
    act_six = gelu_exact(pre_six).astype(jnp.bfloat16)
    joined_six = join_channels(act_six)
    six_pairs = joined_six.reshape(frames, 2 * joined_six.shape[1])
    pre_seven = jnp.dot(six_pairs, weight_seven, preferred_element_type=jnp.float32)
    delta_seven = (masked.astype(jnp.float32) * gelu_slope(pre_seven)).astype(jnp.bfloat16)
    grad_seven = reduce_kernel(six_pairs, delta_seven)
    back_six = spread_channels(
        times_transpose(delta_seven, weight_seven).reshape(2 * frames, full_width)
    )
    delta_six = (back_six * gelu_slope(pre_six)).astype(jnp.bfloat16)
    grad_six = reduce_kernel(in_pairs, delta_six)
    back_in = spread_channels(
        times_transpose(delta_six, weight_six).reshape(4 * frames, full_width)
    )
    grad_features = back_in.astype(jnp.bfloat16)
    return (grad_features, grad_six, grad_seven)


def solution(mesh):
    placed = (P("dp", "mp"), P("dp", "mp"), P("dp", "mp"), P("dp", "mp"), P(), P("dp"))
    return jax.shard_map(
        body,
        mesh=mesh,
        in_specs=placed,
        out_specs=(P("dp", "mp"), P("dp", "mp"), P("dp", "mp")),
        check_vma=False,
    )
```

profile of v0, /device:TPU:0, one launch (start us, length us, event | category | flops | bytes accessed | tf_op | source)
XLA Modules:
  0.0 735.2 jit_solution(9145920384795812149)
XLA Ops:
  8.0 26.4 %all_gather.13 = bf16[1024,128]{1,0:T(8,128)(2,1)S(1)} all-gather(bf16[32,128]{1,0:T(8,128)(2,1)S(1)} %copy-done.4), channel_id=1, replica_groups=mesh['dp'=32,'mp'=4] {'dp'}, dimensions={0}, use_global_device_ids=true | all-gather | bytes 270336 | tf_op jit(solution)/shard_map/all_gather | solution.py:79
  34.4 65.2 %all-gather.3.cloned.1.call-done = bf16[8192,512]{1,0:T(8,128)(2,1)} async-done(((bf16[8192,128]{1,0:T(8,128)(2,1)}), bf16[8192,512]{1,0:T(8,128)(2,1)}) %all-gather.3.cloned.1.call-update) | async-done | bytes 8388624 | tf_op jit(solution)/shard_map/all_gather | solution.py:37
  99.6 12.9 %reshape.258 = bf16[4096,1024]{1,0:T(8,128)(2,1)} reshape(bf16[8192,512]{1,0:T(8,128)(2,1)} %all-gather.3.cloned.1.call-done) | data formatting | bytes 16777216 | tf_op jit(solution)/shard_map/reshape | solution.py:85
  112.5 7.4 %multiply_convert_fusion = (bf16[4096,128]{1,0:T(8,128)(2,1)}, f32[4096,128]{1,0:T(8,128)}) fusion(bf16[4096,1024]{1,0:T(8,128)(2,1)} %reshape.258, bf16[1024,128]{1,0:T(8,128)(2,1)S(1)} %all_gather.13), kind=kOutput, calls=%fused_computation.11 | convolution fusion | flops 1076363264 | bytes 11796480 | tf_op jit(solution)/shard_map/dot_general | solution.py:86
  121.3 5.0 sort.34
  127.0 34.3 %gather_fusion = s32[6144]{0:T(1024)S(1)} fusion(s32[2048]{0:T(1024)S(1)} %get-tuple-element.17, s32[6144]{0:T(1024)S(1)} %broadcast_clamp_fusion), kind=kCustom, calls=%fused_computation | custom fusion | bytes 73728 | tf_op jit(solution)/shard_map/gather | solution.py:59
  161.4 34.3 %gather_fusion.2 = s32[6144]{0:T(1024)S(1)} fusion(s32[2048]{0:T(1024)S(1)} %get-tuple-element.31, s32[6144]{0:T(1024)S(1)} %broadcast_clamp_fusion.1), kind=kCustom, calls=%fused_computation.2 | custom fusion | bytes 73728 | tf_op jit(solution)/shard_map/gather | solution.py:61
  196.5 7.3 all-to-all-start.1
  203.8 18.1 %gather_fusion.1 = bf16[6144,128]{1,0:T(8,128)(2,1)S(1)} fusion(bf16[2048,128]{1,0:T(8,128)(2,1)S(1)} %copy-done, s32[6144]{0:T(1024)S(1)} %broadcast_clamp_fusion.1), kind=kCustom, calls=%fused_computation.1 | custom fusion | bytes 3170304 | tf_op jit(solution)/shard_map/gather | solution.py:60
  224.4 7.5 %all-to-all-start = ((bf16[32,192,128]{2,1,0:T(8,128)(2,1)}), bf16[32,192,128]{2,1,0:T(8,128)(2,1)S(1)}, u32[]{:S(2)}, u32[]{:S(2)}) async-start(bf16[32,192,128]{2,1,0:T(8,128)(2,1)} %broadcast_select_fusion), calls=%async_computation | async-start | bytes 3145728 | tf_op jit(solution)/shard_map/all_to_all | solution.py:63
  232.0 38.6 %all_gather.15 = bf16[1024,128]{1,0:T(8,128)(2,1)S(1)} all-gather(bf16[32,128]{1,0:T(8,128)(2,1)S(1)} %copy-done.5), channel_id=1, replica_groups=mesh['dp'=32,'mp'=4] {'dp'}, dimensions={0}, use_global_device_ids=true | all-gather | bytes 270336 | tf_op jit(solution)/shard_map/all_gather | solution.py:80
  274.0 6.7 sort.35
  280.7 6.2 gather_fusion.3
  287.0 7.1 reshape.259
  298.5 4.0 fusion.21
  302.5 9.3 %reshape.260 = f32[4096,512]{1,0:T(8,128)} reshape(f32[2048,1024]{1,0:T(8,128)} %fusion.21) | data formatting | bytes 16777216 | tf_op jit(solution)/shard_map/reshape | solution.py:94
  311.9 78.9 %reduce-scatter.7.cloned.1.call-done = f32[4096,128]{1,0:T(8,128)} async-done(((f32[4096,512]{1,0:T(8,128)}), f32[4096,128]{1,0:T(8,128)}) %reduce-scatter.7.cloned.1.call-update) | async-done | bytes 2097168 | tf_op jit(solution)/shard_map/reduce_scatter | solution.py:41
  390.8 9.7 %fusion.24 = f32[4096,1024]{1,0:T(8,128)} fusion(bf16[1024,128]{1,0:T(8,128)(2,1)S(1)} %all_gather.13, f32[4096,128]{1,0:T(8,128)} %reduce-scatter.7.cloned.1.call-done, f32[4096,128]{1,0:T(8,128)S(1)} %copy-done.2), kind=kOutput, calls=%fused_computation.51 | convolution fusion | flops 1078984704 | bytes 21233664 | tf_op jit(solution)/shard_map/dot_general | solution.py:31
  400.5 18.2 %reshape.261 = f32[8192,512]{1,0:T(8,128)} reshape(f32[4096,1024]{1,0:T(8,128)} %fusion.24) | data formatting | bytes 33554432 | tf_op jit(solution)/shard_map/reshape | solution.py:99
  418.7 4.9 fusion.19
  423.7 6.6 convolution_bitcast_fusion
  431.4 135.0 %reduce-scatter.9.cloned.1.call-done = f32[8192,128]{1,0:T(8,128)} async-done(((f32[8192,512]{1,0:T(8,128)}), f32[8192,128]{1,0:T(8,128)}) %reduce-scatter.9.cloned.1.call-update) | async-done | bytes 4194320 | tf_op jit(solution)/shard_map/reduce_scatter | solution.py:41
  570.2 77.5 %reduce-scatter.11.cloned.1.call-done = f32[32,128]{1,0:T(8,128)} async-done(((f32[1024,128]{1,0:T(8,128)}), f32[32,128]{1,0:T(8,128)}) %reduce-scatter.11.cloned.1.call-update) | async-done | bytes 16400 | tf_op jit(solution)/shard_map/reduce_scatter | solution.py:22
  647.7 80.7 %reduce-scatter.13.cloned.1.call-done = f32[32,128]{1,0:T(8,128)} async-done(((f32[1024,128]{1,0:T(8,128)}), f32[32,128]{1,0:T(8,128)}) %reduce-scatter.13.cloned.1.call-update) | async-done | bytes 16400
  (64 shorter events, 19.1 us)
Async XLA Ops:
  7.2 196.6 %copy-start = (bf16[2048,128]{1,0:T(8,128)(2,1)S(1)}, bf16[2048,128]{1,0:T(8,128)(2,1)}, u32[]{:S(2)}) copy-start(bf16[2048,128]{1,0:T(8,128)(2,1)} %param.11) | copy-start | bytes 1572868
  7.2 0.8 copy-start.4
  7.2 92.4 %all-gather.3.cloned.1.call-start = ((), (), s32[]{:S(2)}) async-start(), calls=%async_computation.6 | async-start | bytes 10485760 | tf_op jit(solution)/shard_map/all_gather | solution.py:37
  7.9 279.0 %all-gather.5.cloned.1.call-start = ((), (), s32[]{:S(2)}) async-start(), calls=%async_computation.7 | async-start | bytes 5242880 | tf_op jit(solution)/shard_map/all_gather | solution.py:37
  196.5 27.8 %all-to-all-start.1 = ((s32[32,1,192]{2,1,0:T(1,128)}), s32[32,1,192]{2,1,0:T(1,128)S(1)}, u32[]{:S(2)}, u32[]{:S(2)}) async-start(s32[32,1,192]{2,1,0:T(1,128)} %compare_select_fusion), calls=%async_computation.1 | async-start | bytes 65536 | tf_op jit(solution)/shard_map/all_to_all | solution.py:64
  224.3 7.6 %copy-start.5 = (bf16[32,128]{1,0:T(8,128)(2,1)S(1)}, bf16[32,128]{1,0:T(8,128)(2,1)}, u32[]{:S(2)}) copy-start(bf16[32,128]{1,0:T(8,128)(2,1)} %param.10) | copy-start | bytes 24580
  224.3 46.2 %copy-start.9 = (s32[4]{0:T(128)S(1)}, s32[4]{0:T(128)}, u32[]{:S(2)}) copy-start(s32[4]{0:T(128)} %param.13) | copy-start | bytes 52
  224.3 46.9 %copy-start.6 = (pred[2048]{0:T(1024)(128)(4,1)S(1)}, pred[2048]{0:T(1024)(128)(4,1)}, u32[]{:S(2)}) copy-start(pred[2048]{0:T(1024)(128)(4,1)} %constant.191) | copy-start | bytes 6148
  224.3 46.9 %copy-start.7 = (pred[2048]{0:T(1024)(128)(4,1)S(1)}, pred[2048]{0:T(1024)(128)(4,1)}, u32[]{:S(2)}) copy-start(pred[2048]{0:T(1024)(128)(4,1)} %constant.190) | copy-start | bytes 6148
  224.3 46.9 %copy-start.8 = (pred[2048]{0:T(1024)(128)(4,1)S(1)}, pred[2048]{0:T(1024)(128)(4,1)}, u32[]{:S(2)}) copy-start(pred[2048]{0:T(1024)(128)(4,1)} %constant.189) | copy-start | bytes 6148
  224.4 56.4 %all-to-all-start = ((bf16[32,192,128]{2,1,0:T(8,128)(2,1)}), bf16[32,192,128]{2,1,0:T(8,128)(2,1)S(1)}, u32[]{:S(2)}, u32[]{:S(2)}) async-start(bf16[32,192,128]{2,1,0:T(8,128)(2,1)} %broadcast_select_fusion), calls=%async_computation | async-start | bytes 3145728 | tf_op jit(solution)/shard_map/all_to_all | solution.py:63
  231.9 158.9 %reduce-scatter.7.cloned.1.call-start = ((), (), s32[]{:S(2)}) async-start(), calls=%async_computation.8 | async-start | bytes 10485760 | tf_op jit(solution)/shard_map/reduce_scatter | solution.py:41
  297.5 1.0 copy-start.3
  311.8 79.0 %copy-start.2 = (f32[4096,128]{1,0:T(8,128)S(1)}, f32[4096,128]{1,0:T(8,128)}, u32[]{:S(2)}) copy-start(f32[4096,128]{1,0:T(8,128)} %get-tuple-element.38) | copy-start | bytes 6291460
  311.9 254.6 %reduce-scatter.9.cloned.1.call-start = ((), (), s32[]{:S(2)}) async-start(), calls=%async_computation.9 | async-start | bytes 20971520 | tf_op jit(solution)/shard_map/reduce_scatter | solution.py:41
  418.7 229.0 %reduce-scatter.11.cloned.1.call-start = ((), (), s32[]{:S(2)}) async-start(), calls=%async_computation.10 | async-start | bytes 540672 | tf_op jit(solution)/shard_map/reduce_scatter | solution.py:22
  423.7 304.6 %reduce-scatter.13.cloned.1.call-start = ((), (), s32[]{:S(2)}) async-start(), calls=%async_computation.11 | async-start | bytes 540672
  431.4 296.9 %copy-start.1 = (bf16[2048,128]{1,0:T(8,128)(2,1)S(1)}, bf16[2048,128]{1,0:T(8,128)(2,1)}, u32[]{:S(2)}) copy-start(bf16[2048,128]{1,0:T(8,128)(2,1)} %param.11) | copy-start | bytes 1572868
Sparse Core Ops, SparseCore 0:
  9.7 89.8 all-gather.2
  120.0 52.3 all-gather.4
  312.0 78.8 reduce-scatter.6
  418.8 147.6 reduce-scatter.8
  570.7 76.8 reduce-scatter.10
  651.9 76.3 reduce-scatter.12
where the time goes:
time: 737 us; the launch traced here: 735 us
  waiting for transfers between devices  438 us (59%)
  local copies, waits for them, and re-layouts  144 us (20%)
  blocking collectives  65 us (9%)
  matrix products  36.1 us (5%)
  other arithmetic  23.1 us (3%)
  starting transfers between devices  15 us (2%)
  between operations  14.3 us (2%)
    reduce_scatter x2, waiting for transfers between devices, spread_channels(): return lax.psum_scatter(values, 'mp', scatter_dimension=1, tiled=True)  214 us
    unnamed x7, waiting for transfers between devices  81.4 us
    reduce_scatter x1, waiting for transfers between devices, reduce_kernel(): lax.psum_scatter(lax.dot_general(left, right, (((0,), (0,)), ((), ())), p...  77.5 us
    all_gather x2, waiting for transfers between devices, join_channels(): return lax.all_gather(values, 'mp', axis=1, tiled=True)  65.2 us
    all_gather x1, blocking collectives, body(): lax.all_gather(conv7_weight, 'dp', axis=0, tiled=True)  38.6 us
    gather x2, local copies, waits for them, and re-layouts, route_frames(): target_rows = jnp.where(filled, own_rows[source_row], frames)  34.4 us
    gather x2, local copies, waits for them, and re-layouts, route_frames(): source_row = grouped[pick_index]  34.4 us
    all_gather x1, blocking collectives, body(): lax.all_gather(conv6_weight, 'dp', axis=0, tiled=True)  26.4 us
  transfers between devices with their start and end apart: 8, of which 5 were waited for; matrix products, arithmetic and copies ran while one was open for 18% of the time, Pallas kernels for 0%

commit v1 on v0

v1 whole, which is shorter than its diff:
```python
import jax
import jax.numpy as jnp
from jax import lax
from jax.experimental import pallas as pl
from jax.experimental.pallas import tpu as pltpu
from jax.sharding import PartitionSpec as P

C = 512
FRM = 2048
CAP = 192
N_DP = 32
N_MP = 4
CH = C // N_MP
UTT = FRM // N_MP
FC = 128
NCH = UTT // FC
RC = 4 * FC
META = 16
BLK = CAP + META
SLOT = 256
GRP = 4
KR = 32
NQ = N_DP // 2

inv_root_two = 0.7071067811865476
inv_root_tau = 0.3989422804014327
F32 = jnp.float32
BF16 = jnp.bfloat16


def dot(left, right, contract=((1,), (0,))):
    return lax.dot_general(left, right, (contract, ((), ())), preferred_element_type=F32)


def iota(shape, axis):
    return lax.broadcasted_iota(jnp.int32, shape, axis)


def kernel(
    feat, w6, w7, grads, dest, lens,
    gf, g6, g7,
    xin, wts, rank, rhs, obox, arrived, placed, exb, mg,
    s32, pairs6, pairs7, slope6, slope7, delta7, delta6, gout,
    gsum, core_out, core_in, chip_in, chip_out, share, x_out, x_in,
    wx_s, wx_r, wy_s, wy_r, wc_s, wc_r, own_sem, f_s, f_r, rt_s, rt_r, ex_s, ex_r,
    go_s, go_r, rc_s, rc_r, ry_s, ry_r, rx_s, rx_r,
):
    d, m = lax.axis_index("dp"), lax.axis_index("mp")
    core, q = lax.rem(d, 2), lax.div(d, 2)
    mate = d + 1 - 2 * core

    def remote(src, dst, send, recv, dp, mp):
        return pltpu.make_async_remote_copy(
            src_ref=src, dst_ref=dst, send_sem=send, recv_sem=recv,
            device_id=(dp, mp), device_id_type=pl.DeviceIdType.MESH,
        )

    barrier = pltpu.get_barrier_semaphore()

    @pl.loop(1, N_DP)
    def _(k):
        pl.semaphore_signal(barrier, inc=1, device_id=(lax.rem(d + k, N_DP), m), device_id_type=pl.DeviceIdType.MESH)

    for i in range(1, N_MP):
        pl.semaphore_signal(barrier, inc=1, device_id=(d, lax.rem(m + i, N_MP)), device_id_type=pl.DeviceIdType.MESH)
    pl.semaphore_wait(barrier, N_DP - 1 + N_MP - 1)

    cols = pl.ds(pl.multiple_of(m * CH, CH), CH)
    wts[0, q, core, :, cols] = w6[...]
    wts[1, q, core, :, cols] = w7[...]

    def wx(i, w):
        block = wts.at[w, q, core, :, cols]
        return remote(block, block, wx_s.at[i, w], wx_r.at[i, w], d, lax.rem(m + i, N_MP))

    for i in range(1, N_MP):
        for w in range(2):
            wx(i, w).start()

    def feature(c, i):
        p = lax.rem(m + i, N_MP)
        return remote(
            feat.at[pl.ds(pl.multiple_of(p * 4 * UTT + c * RC, RC), RC), :],
            xin.at[m, pl.ds(pl.multiple_of(c * RC, RC), RC), :],
            f_s.at[c, i], f_r.at[c, i], d, p,
        )

    own_rows = pltpu.make_async_copy(
        feat.at[pl.ds(pl.multiple_of(m * 4 * UTT, 4 * UTT), 4 * UTT), :], xin.at[m], own_sem.at[0]
    )
    own_rows.start()

    for c in range(NCH):
        for i in range(1, N_MP):
            feature(c, i).start()

    target = dest[...]
    owner, row = lax.shift_right_logical(target, 11), lax.bitwise_and(target, FRM - 1)
    before = jnp.where(iota((256, 256), 0) < iota((256, 256), 1), 1.0, 0.0).astype(BF16)
    carry = jnp.zeros((N_DP, 1), F32)
    for b in range(FRM // 256):
        mine = owner[:, b * 256 : (b + 1) * 256] == iota((N_DP, 256), 0)
        ones = jnp.where(mine, 1.0, 0.0)
        earlier = dot(ones.astype(BF16), before) + carry
        rank[:, b * 256 : (b + 1) * 256] = jnp.where(mine, earlier.astype(jnp.int32), 4096)
        carry = carry + jnp.sum(ones, axis=1, keepdims=True)
    high, low = lax.shift_right_logical(row, 8), lax.bitwise_and(row, 255)
    rhs[:, 0:CH] = grads[...]
    for b in range(FRM // 128):
        part = slice(b * 128, (b + 1) * 128)
        line = iota((128, 128), 0)
        digits = jnp.where(line == 0, high[:, part], jnp.where(line == 1, low[:, part], 0))
        rhs[part, CH : 2 * CH] = digits.astype(F32).T.astype(BF16)

    for i in range(1, N_MP):
        for w in range(2):
            wx(i, w).wait()

    def wy(k):
        block = wts.at[:, q, core]
        return remote(block, block, wy_s.at[k], wy_r.at[k], 2 * lax.rem(q + k, NQ) + core, m)

    @pl.loop(1, NQ)
    def _(k):
        wy(k).start()

    def routed(k):
        return remote(
            obox.at[k], arrived.at[k, pl.ds(0, BLK), :], rt_s.at[k], rt_r.at[k], lax.rem(d + k, N_DP), m
        )

    arrived[:, BLK:SLOT, :] = jnp.zeros((N_DP, SLOT - BLK, CH), BF16)

    def pack(k):
        o = lax.rem(d + k, N_DP)
        pick = jnp.where(iota((CAP, FRM), 0) == rank[pl.ds(o, 1), :], 1.0, 0.0).astype(BF16)
        both = dot(pick, rhs[...])
        obox[k, 0:CAP, :] = both[:, :CH].astype(BF16)
        digits = jnp.concatenate([both[:, CH:], jnp.zeros((SLOT - CAP, CH), F32)], axis=0).T
        obox[k, CAP:BLK, :] = jnp.concatenate([digits[0:8, 0:128], digits[0:8, 128:256]], axis=0).astype(BF16)

    @pl.loop(1, N_DP)
    def _(k):
        pack(k)
        routed(k).start()

    pack(0)
    arrived[0, 0:BLK, :] = obox[0]

    @pl.loop(1, NQ)
    def _(k):
        wy(k).wait()

    def wc(w):
        block = wts.at[w, :, core]
        return remote(block, block, wc_s.at[w], wc_r.at[w], mate, m)

    for w in range(2):
        wc(w).start()

    def place(g):
        targets = []
        for i in range(GRP):
            digits = arrived[g * GRP + i, CAP:BLK, :].astype(F32)
            targets += [
                digits[0:1] * 256.0 + digits[1:2],
                jnp.where(iota((1, 128), 1) < CAP - 128, digits[8:9] * 256.0 + digits[9:10], -1.0),
            ]
        at = jnp.concatenate(targets, axis=1).astype(jnp.int32)
        block = arrived[pl.ds(g * GRP, GRP)].reshape(GRP * SLOT, CH)

        @pl.loop(0, N_MP)
        def _(p):
            pick = jnp.where(iota((UTT, GRP * SLOT), 0) == at - p * UTT, 1.0, 0.0).astype(BF16)
            placed[p] += dot(pick, block)

    placed[...] = jnp.zeros((N_MP, UTT, CH), F32)
    for w in range(2):
        wc(w).wait()
    own_rows.wait()

    def forward(c):
        rows = pl.ds(pl.multiple_of(c * RC, RC), RC)
        for g in range(N_MP):
            s32[g] = xin[g, rows, :].astype(F32)
        for j in range(4):
            for g in range(N_MP):
                lanes = slice((j % 2) * C + g * CH, (j % 2) * C + (g + 1) * CH)
                pairs6[c, (j // 2) * FC : (j // 2 + 1) * FC, lanes] = s32[g, pl.ds(j, FC, stride=4), :].astype(BF16)
        pre = dot(pairs6[c], wts[0].reshape(2 * C, C))
        half = 0.5 * (1.0 + lax.erf(pre * inv_root_two))
        act = (pre * half).astype(BF16)
        slope6[c] = half + pre * jnp.exp(-0.5 * pre * pre) * inv_root_tau
        pairs7[c, :, 0:C] = act[:FC]
        pairs7[c, :, C : 2 * C] = act[FC:]
        pre = dot(pairs7[c], wts[1].reshape(2 * C, C))
        half = 0.5 * (1.0 + lax.erf(pre * inv_root_two))
        slope7[c] = half + pre * jnp.exp(-0.5 * pre * pre) * inv_root_tau

    @pl.loop(0, NCH)
    def _(c):
        for i in range(1, N_MP):
            feature(c, i).wait()
        forward(c)

    for i in range(1, GRP):
        routed(i).wait()
    place(0)

    @pl.loop(1, N_DP // GRP)
    def _(g):
        for i in range(GRP):
            routed(g * GRP + i).wait()
        place(g)

    def exchange(i):
        p = lax.rem(m + i, N_MP)
        return remote(exb.at[p], mg.at[m], ex_s.at[i], ex_r.at[i], d, p)

    exb[...] = placed[...].astype(BF16)
    for i in range(1, N_MP):
        exchange(i).start()
    mg[m] = exb[m]
    for i in range(1, N_MP):
        exchange(i).wait()

    valid = lax.div(lens[m] - 400, 320) + 1

    def given(c, i):
        p = lax.rem(m + i, N_MP)
        return remote(
            gout.at[p, pl.ds(pl.multiple_of(c * RC, RC), RC), :],
            gf.at[pl.ds(pl.multiple_of(m * 4 * UTT + c * RC, RC), RC), :],
            go_s.at[c, i], go_r.at[c, i], d, p,
        )

    def own_given(c):
        return pltpu.make_async_copy(
            gout.at[m, pl.ds(pl.multiple_of(c * RC, RC), RC), :],
            gf.at[pl.ds(pl.multiple_of(m * 4 * UTT + c * RC, RC), RC), :],
            go_s.at[c, 0],
        )

    @pl.loop(0, NCH)
    def _(c):
        frames = pl.ds(pl.multiple_of(c * FC, FC), FC)
        live = iota((FC, CH), 0) + c * FC < valid
        for g in range(N_MP):
            lanes = slice(g * CH, (g + 1) * CH)
            coming = jnp.where(live, mg[g, frames, :].astype(F32), 0.0)
            delta7[c, :, lanes] = (coming * slope7[c, :, lanes]).astype(BF16)
        back = dot(delta7[c], wts[1].reshape(2 * C, C), ((1,), (1,)))
        delta6[c, 0:FC, :] = (back[:, :C] * slope6[c, 0:FC, :]).astype(BF16)
        delta6[c, FC : 2 * FC, :] = (back[:, C:] * slope6[c, FC : 2 * FC, :]).astype(BF16)
        back = dot(delta6[c], wts[0].reshape(2 * C, C), ((1,), (1,)))
        for j in range(4):
            for g in range(N_MP):
                s32[g, pl.ds(j, FC, stride=4), :] = back[
                    (j // 2) * FC : (j // 2 + 1) * FC, (j % 2) * C + g * CH : (j % 2) * C + (g + 1) * CH
                ]
        for g in range(N_MP):
            gout[g, pl.ds(pl.multiple_of(c * RC, RC), RC), :] = s32[g].astype(BF16)
        for i in range(1, N_MP):
            given(c, i).start()
        own_given(c).start()

    @pl.loop(0, 2 * C // 256)
    def _(b):
        lanes = pl.ds(pl.multiple_of(b * 256, 256), 256)
        blocks = pl.ds(b * 4, 4)
        left = pairs7[:, :, lanes].reshape(UTT, 256)
        right = delta7[...].reshape(UTT, C)
        gsum[1, blocks] = dot(left, right, ((0,), (0,))).reshape(4, 2, KR, C)
        left = pairs6[:, :, lanes].reshape(2 * UTT, 256)
        right = delta6[...].reshape(2 * UTT, C)
        gsum[0, blocks] = dot(left, right, ((0,), (0,))).reshape(4, 2, KR, C)

    core_out[...] = gsum[:, :, 1 - core].astype(BF16)
    to_mate = remote(core_out, core_in, rc_s.at[0], rc_r.at[0], mate, m)
    to_mate.start()
    to_mate.wait()

    def chips(k):
        o = lax.rem(q + k, NQ)
        return remote(chip_out.at[o], chip_in.at[k], ry_s.at[k], ry_r.at[k], 2 * o + core, m)

    @pl.loop(0, NQ)
    def _(o):
        for w in range(2):
            chip_out[o, w] = (gsum[w, o, core] + core_in[w, o].astype(F32)).astype(BF16)

    @pl.loop(1, NQ)
    def _(k):
        chips(k).start()

    for w in range(2):
        share[w] = gsum[w, q, core] + core_in[w, q].astype(F32)

    @pl.loop(1, NQ)
    def _(k):
        chips(k).wait()
        share[...] += chip_in[k].astype(F32)

    for g in range(N_MP):
        x_out[g] = share[:, :, g * CH : (g + 1) * CH].astype(BF16)

    def along(i):
        p = lax.rem(m + i, N_MP)
        return remote(x_out.at[p], x_in.at[i], rx_s.at[i], rx_r.at[i], d, p)

    for i in range(1, N_MP):
        along(i).start()
    total = jnp.zeros((2, KR, CH), F32)
    for g in range(N_MP):
        total = jnp.where(m == g, share[:, :, g * CH : (g + 1) * CH], total)
    for i in range(1, N_MP):
        along(i).wait()
        total = total + x_in[i].astype(F32)
    g6[...] = total[0]
    g7[...] = total[1]

    @pl.loop(0, NCH)
    def _(c):
        for i in range(1, N_MP):
            given(c, i).wait()
        own_given(c).wait()


def body(features, conv6_weight, conv7_weight, frame_grads, frame_dest, lengths):
    d = lax.axis_index("dp")
    own = lax.dynamic_slice_in_dim(frame_dest, d * FRM, FRM, 0).reshape(1, FRM)
    vmem, hbm = pl.BlockSpec(memory_space=pltpu.VMEM), pl.BlockSpec(memory_space=pl.ANY)
    dma = pltpu.SemaphoreType.DMA
    return pl.pallas_call(
        kernel,
        out_shape=(
            jax.ShapeDtypeStruct(features.shape, BF16),
            jax.ShapeDtypeStruct(conv6_weight.shape, F32),
            jax.ShapeDtypeStruct(conv7_weight.shape, F32),
        ),
        in_specs=[hbm, vmem, vmem, vmem, vmem, pl.BlockSpec(memory_space=pltpu.SMEM)],
        out_specs=(hbm, vmem, vmem),
        scratch_shapes=[
            pltpu.VMEM((N_MP, 4 * UTT, CH), BF16),
            pltpu.VMEM((2, NQ, 2, KR, C), BF16),
            pltpu.VMEM((N_DP, FRM), jnp.int32),
            pltpu.VMEM((FRM, 2 * CH), BF16),
            pltpu.VMEM((N_DP, BLK, CH), BF16),
            pltpu.VMEM((N_DP, SLOT, CH), BF16),
            pltpu.VMEM((N_MP, UTT, CH), F32),
            pltpu.VMEM((N_MP, UTT, CH), BF16),
            pltpu.VMEM((N_MP, UTT, CH), BF16),
            pltpu.VMEM((N_MP, RC, CH), F32),
            pltpu.VMEM((NCH, 2 * FC, 2 * C), BF16),
            pltpu.VMEM((NCH, FC, 2 * C), BF16),
            pltpu.VMEM((NCH, 2 * FC, C), F32),
            pltpu.VMEM((NCH, FC, C), F32),
            pltpu.VMEM((NCH, FC, C), BF16),
            pltpu.VMEM((NCH, 2 * FC, C), BF16),
            pltpu.VMEM((N_MP, 4 * UTT, CH), BF16),
            pltpu.VMEM((2, NQ, 2, KR, C), F32),
            pltpu.VMEM((2, NQ, KR, C), BF16),
            pltpu.VMEM((2, NQ, KR, C), BF16),
            pltpu.VMEM((NQ, 2, KR, C), BF16),
            pltpu.VMEM((NQ, 2, KR, C), BF16),
            pltpu.VMEM((2, KR, C), F32),
            pltpu.VMEM((N_MP, 2, KR, CH), BF16),
            pltpu.VMEM((N_MP, 2, KR, CH), BF16),
            dma((N_MP, 2)), dma((N_MP, 2)), dma((NQ,)), dma((NQ,)), dma((2,)), dma((2,)), dma((1,)),
            dma((NCH, N_MP)), dma((NCH, N_MP)), dma((N_DP,)), dma((N_DP,)), dma((N_MP,)), dma((N_MP,)),
            dma((NCH, N_MP)), dma((NCH, N_MP)), dma((1,)), dma((1,)), dma((NQ,)), dma((NQ,)),
            dma((N_MP,)), dma((N_MP,)),
        ],
        compiler_params=pltpu.CompilerParams(
            collective_id=0, has_side_effects=True, vmem_limit_bytes=56 * 2**20,
            fuse_transposed_lhs_in_matmul=True,
        ),
        name="encoder_backward",
    )(features, conv6_weight, conv7_weight, frame_grads, own, lengths)


def solution(mesh):
    placed = (P("dp", "mp"), P("dp", "mp"), P("dp", "mp"), P("dp", "mp"), P(), P("dp"))
    return jax.shard_map(
        body,
        mesh=mesh,
        in_specs=placed,
        out_specs=(P("dp", "mp"), P("dp", "mp"), P("dp", "mp")),
        check_vma=False,
    )
```

time: 737 us -> 106 us (0.14)
  waiting for transfers between devices: 438 us -> 0 us
  local copies, waits for them, and re-layouts: 144 us -> 5.57 us
  Pallas kernels: 0 us -> 99.1 us
  blocking collectives: 65 us -> 0 us
  matrix products: 36.1 us -> 0 us
  other arithmetic: 23.1 us -> 0 us
  starting transfers between devices: 15 us -> 0 us
  between operations: 14.3 us -> 0.66 us
    reduce_scatter x3 -> x0, waiting for transfers between devices: 291 us -> none  [the longest x2 214 us: spread_channels(): return lax.psum_scatter(values, 'mp', scatter_dimension=1, tiled=True)]
    pallas_call x0 -> x1, Pallas kernels: none -> 99.1 us  [body(): pl.pallas_call(kernel, out_shape=(jax.ShapeDtypeStruct(features.shape, BF...]
    gather x7 -> x0, local copies, waits for them, and re-layouts: 93.7 us -> none  [the longest x2 34.4 us: route_frames(): target_rows = jnp.where(filled, own_rows[source_row], frames)]
    unnamed x7 -> x0, waiting for transfers between devices: 81.4 us -> none
    all_gather x2 -> x0, waiting for transfers between devices: 65.2 us -> none  [join_channels(): return lax.all_gather(values, 'mp', axis=1, tiled=True)]
    all_gather x2 -> x0, blocking collectives: 65 us -> none  [the longest x1 38.6 us: body(): lax.all_gather(conv7_weight, 'dp', axis=0, tiled=True)]
    reshape x5 -> x0, local copies, waits for them, and re-layouts: 47.5 us -> none  [the longest x1 18.2 us: body(): times_transpose(delta_six, weight_six).reshape(4 * frames, full_width)]
    dot_general x6 -> x0, matrix products: 36.1 us -> none  [the longest x2 13.6 us: times_transpose(): lax.dot_general(left, right, (((1,), (1,)), ((), ())), preferred_element_...]
  transfers between devices with their start and end apart: 8 -> 0, of which waited for: 5 -> 0; matrix products, arithmetic and copies ran while one was open for 18% -> 0% of each run, Pallas kernels for 0% -> 0%
where the time goes in v1:
time: 106 us; the launch traced here: 105 us
  Pallas kernels  99.1 us (93%)
  local copies, waits for them, and re-layouts  5.57 us (5%)
    pallas_call x1, Pallas kernels, body(): pl.pallas_call(kernel, out_shape=(jax.ShapeDtypeStruct(features.shape, BF...  99.1 us
    unnamed x7, local copies, waits for them, and re-layouts  4.27 us

profile of v1, /device:TPU:0, one launch (start us, length us, event | category | flops | bytes accessed | tf_op | source)
XLA Modules:
  0.0 105.3 jit_solution(17575022083439637567)
XLA Ops:
  0.6 1.3 %dynamic_slice.3 = s32[2048]{0:T(1024)} dynamic-slice(s32[65536]{0:T(1024)} %param.10, s32[]{:T(128)S(6)} %select_n.3), dynamic_slice_sizes={2048} | dynamic-slice | bytes 16388 | tf_op jit(solution)/shard_map/dynamic_slice | solution.py:331
  1.9 99.1 %encoder_backward.1 = (bf16[8192,128]{1,0:T(8,128)(2,1)}, f32[32,128]{1,0:T(8,128)}, f32[32,128]{1,0:T(8,128)}) custom-call(bf16[8192,128]{1,0:T(8,128)(2,1)} %feat.1, bf16[32,128]{1,0:T(8,128)(2,1)} %w6.1, bf16[32,128]{1,0:T(8,128)(2,1)} %w7.1, bf16[2048,128]{1,0:T(8,128)(2,1)} %grads.1, s32[1,2048]{1,0:T(1,128)} %bitcast.1, s32[4]{0:T(128)} %lens.1), custom_call_target="tpu_custom_call" | custom-call | tf_op jit(solution)/shard_map/encoder_backward/pallas_call | solution.py:334
  101.1 0.0 copy-start.1
  101.1 0.0 copy-start
  101.1 3.1 %copy.12 = bf16[8192,128]{1,0:T(8,128)(2,1)} copy(bf16[8192,128]{1,0:T(8,128)(2,1)} %get-tuple-element.6) | data formatting | bytes 4194304
  104.1 0.0 copy-done.1
  104.1 0.6 copy.13
  104.7 0.0 copy-done
  104.7 0.6 copy.14
Async XLA Ops:
  101.1 3.1 %copy-start.1 = (f32[32,128]{1,0:T(8,128)S(1)}, f32[32,128]{1,0:T(8,128)}, u32[]{:S(2)}) copy-start(f32[32,128]{1,0:T(8,128)} %get-tuple-element.7) | copy-start | bytes 49156
  101.1 3.7 %copy-start = (f32[32,128]{1,0:T(8,128)S(1)}, f32[32,128]{1,0:T(8,128)}, u32[]{:S(2)}) copy-start(f32[32,128]{1,0:T(8,128)} %get-tuple-element.8) | copy-start | bytes 49156

commit v2 on v1

v2 whole, which is shorter than its diff:
```python
import jax
import jax.numpy as jnp
from jax import lax
from jax.experimental import pallas as pl
from jax.experimental.pallas import tpu as pltpu
from jax.sharding import PartitionSpec as P

C = 512
FRM = 2048
CAP = 192
N_DP = 32
N_MP = 4
CH = C // N_MP
UTT = FRM // N_MP
FC = 128
NCH = UTT // FC
RC = 4 * FC
META = 16
BLK = CAP + META
KR = 32

inv_root_two = 0.7071067811865476
inv_root_tau = 0.3989422804014327
F32 = jnp.float32
BF16 = jnp.bfloat16


def dot(left, right, contract=((1,), (0,))):
    return lax.dot_general(left, right, (contract, ((), ())), preferred_element_type=F32)


def iota(shape, axis):
    return lax.broadcasted_iota(jnp.int32, shape, axis)


def kernel(
    feat, w6, w7, grads, dest, lens,
    gf, g6, g7,
    xin, wts, quad, meta, rhs, obox, arrived, placed, exb, mg,
    s32, pairs6, pairs7, slope6, slope7, delta7, delta6, gout,
    gsum, core_out, core_in, part_out, part_in, part, chip_out, chip_in, share, x_out, x_in,
    wx_s, wx_r, wa_s, wa_r, wb_s, wb_r, wc_s, wc_r, own_sem, f_s, f_r, rt_s, rt_r, ex_s, ex_r,
    go_s, go_r, rc_s, rc_r, ra_s, ra_r, rb_s, rb_r, rx_s, rx_r,
):
    d, m = lax.axis_index("dp"), lax.axis_index("mp")
    z, y, core = lax.div(d, 8), lax.rem(lax.div(d, 2), 4), lax.rem(d, 2)

    def dp_of(dz, dy, dc):
        return lax.rem(z + dz, 4) * 8 + lax.rem(y + dy, 4) * 2 + lax.rem(core + dc, 2)

    def remote(src, dst, send, recv, dp, mp):
        return pltpu.make_async_remote_copy(
            src_ref=src, dst_ref=dst, send_sem=send, recv_sem=recv,
            device_id=(dp, mp), device_id_type=pl.DeviceIdType.MESH,
        )

    barrier = pltpu.get_barrier_semaphore()
    for i in range(1, N_MP):
        pl.semaphore_signal(barrier, inc=1, device_id=(d, lax.rem(m + i, N_MP)), device_id_type=pl.DeviceIdType.MESH)

    @pl.loop(1, N_DP)
    def _(k):
        pl.semaphore_signal(barrier, inc=1, device_id=(lax.rem(d + k, N_DP), m), device_id_type=pl.DeviceIdType.MESH)

    own_rows = pltpu.make_async_copy(
        feat.at[pl.ds(pl.multiple_of(m * 4 * UTT, 4 * UTT), 4 * UTT), :], xin.at[m], own_sem.at[0]
    )
    own_rows.start()
    cols = pl.ds(pl.multiple_of(m * CH, CH), CH)
    wts[0, z, y, core, :, cols] = w6[...]
    wts[1, z, y, core, :, cols] = w7[...]
    pl.semaphore_wait(barrier, N_DP - 1 + N_MP - 1)

    def wx(i, w):
        block = wts.at[w, z, y, core, :, cols]
        return remote(block, block, wx_s.at[i, w], wx_r.at[i, w], d, lax.rem(m + i, N_MP))

    for i in range(1, N_MP):
        for w in range(2):
            wx(i, w).start()

    def feature(c, i):
        p = lax.rem(m + i, N_MP)
        return remote(
            feat.at[pl.ds(pl.multiple_of(p * 4 * UTT + c * RC, RC), RC), :],
            xin.at[m, pl.ds(pl.multiple_of(c * RC, RC), RC), :],
            f_s.at[c, i], f_r.at[c, i], d, p,
        )

    for c in range(NCH):
        for i in range(1, N_MP):
            feature(c, i).start()

    def number_slots():
        target = dest[...]
        row = lax.bitwise_and(target, FRM - 1)
        shifted = lambda by, top: lax.bitwise_and(lax.shift_right_logical(target, by), top)
        owner = (
            lax.bitwise_and(shifted(14, 3) - z, 3) * 8
            + lax.bitwise_and(shifted(12, 3) - y, 3) * 2
            + lax.bitwise_and(shifted(11, 1) + core, 1)
        )
        before = jnp.where(iota((256, 256), 0) < iota((256, 256), 1), 1.0, 0.0).astype(BF16)
        carry = jnp.zeros((N_DP, 1), F32)
        ranks = []
        for b in range(FRM // 256):
            mine = owner[:, b * 256 : (b + 1) * 256] == iota((N_DP, 256), 0)
            ones = jnp.where(mine, 1.0, 0.0)
            earlier = dot(ones.astype(BF16), before) + carry
            ranks.append(jnp.sum(jnp.where(mine, earlier, 0.0), axis=0, keepdims=True))
            carry = carry + jnp.sum(ones, axis=1, keepdims=True)
        rank = jnp.concatenate(ranks, axis=1).astype(jnp.int32)
        quad[...] = jnp.where(lax.shift_right_logical(owner, 2) == iota((8, FRM), 0), rank, 4096)
        remainder = jnp.where(lax.bitwise_and(owner, 3) == iota((8, FRM), 0), 1.0, 0.0).astype(BF16)
        spread = jnp.where(iota((8, 4 * CH), 0) == lax.div(iota((8, 4 * CH), 1), CH), 1.0, 0.0).astype(BF16)
        for b in range(FRM // 256):
            part_ = slice(b * 256, (b + 1) * 256)
            keep = dot(remainder[:, part_], spread, ((0,), (0,))).astype(BF16)
            rows = grads[part_, :]
            rhs[part_, :] = keep * jnp.concatenate([rows] * 4, axis=1)
        line = iota((2 * N_DP, FRM), 0)
        digits = jnp.where(
            line == owner, lax.shift_right_logical(row, 8),
            jnp.where(line == owner + N_DP, lax.bitwise_and(row, 255), 0),
        ).astype(F32).astype(BF16)
        for odd in range(2):
            pick = jnp.where(iota((256, FRM), 0) == rank + 64 * odd, 1.0, 0.0).astype(BF16)
            meta[odd] = dot(digits, pick, ((1,), (1,)))

    number_slots()

    def routed(k):
        return remote(
            obox.at[k], arrived.at[k], rt_s.at[k], rt_r.at[k],
            dp_of(lax.div(k, 8), lax.rem(lax.div(k, 2), 4), lax.rem(k, 2)), m,
        )

    own_block = pltpu.make_async_copy(obox.at[0], arrived.at[0], rt_r.at[0])

    def pack(g):
        pick = jnp.where(iota((CAP, FRM), 0) == quad[pl.ds(g, 1), :], 1.0, 0.0).astype(BF16)
        both = dot(pick, rhs[...])
        line = iota((META, 128), 0)
        for j in range(4):
            k = g * 4 + j
            obox[k, 0:CAP, :] = both[:, j * CH : (j + 1) * CH].astype(BF16)
            high, low = meta[j % 2, pl.ds(k, 1), :], meta[j % 2, pl.ds(k + N_DP, 1), :]
            tile = jnp.where(line == 0, high[:, :128], jnp.where(line == 1, high[:, 128:], 0.0))
            tile = jnp.where(line == 2, low[:, :128], jnp.where(line == 3, low[:, 128:], tile))
            obox[k, CAP:BLK, :] = tile.astype(BF16)

    @pl.loop(0, 8)
    def _(i):
        g = lax.rem(5 * i + 2, 8)
        pack(g)
        for j in range(1, 4):
            routed(g * 4 + j).start()

        @pl.when(g != 0)
        def _():
            routed(g * 4).start()

        @pl.when(g == 0)
        def _():
            own_block.start()

    for i in range(1, N_MP):
        for w in range(2):
            wx(i, w).wait()

    def along_z(i):
        return dp_of(i, 0, 0)

    def along_y(i):
        return dp_of(0, i, 0)

    def wa(w, i):
        block = wts.at[w, z, y, core]
        return remote(block, block, wa_s.at[w, i], wa_r.at[w, i], (along_z, along_y)[w](i), m)

    def wb(w, i):
        block = wts.at[0, :, y, core] if w == 0 else wts.at[1, z, :, core]
        return remote(block, block, wb_s.at[w, i], wb_r.at[w, i], (along_y, along_z)[w](i), m)

    def wc(w):
        block = wts.at[w, :, :, core]
        return remote(block, block, wc_s.at[w], wc_r.at[w], dp_of(0, 0, 1), m)

    for w in range(2):
        for i in range(1, 4):
            wa(w, i).start()

    def place(g):
        first, second = [], []
        for i in range(4):
            digits = arrived[g * 4 + i, CAP:BLK, :].astype(F32)
            first.append(digits[0:1] * 256.0 + digits[2:3])
            second.append(digits[1:2] * 256.0 + digits[3:4])
        left = iota((1, 128), 1) < 64
        at = jnp.concatenate(
            [
                first[0], jnp.where(left, second[0], first[1]), second[1],
                first[2], jnp.where(left, second[2], first[3]), second[3],
            ],
            axis=1,
        ).astype(jnp.int32)
        half = lax.shift_right_logical(at, 10)
        within = lax.bitwise_and(at, 1023)
        top = jnp.where(iota((8, 4 * CAP), 0) == 0, half, 0).astype(F32).astype(BF16)
        later = dot(top, jnp.ones((8, CH), BF16), ((0,), (0,))).astype(BF16)
        block = arrived[pl.ds(g * 4, 4), 0:CAP, :].reshape(4 * CAP, CH)
        second_half = block * later
        sides = jnp.concatenate([block - second_half, second_half], axis=1)
        for a in range(2):
            pick = jnp.where(iota((UTT, 4 * CAP), 0) + a * UTT == within, 1.0, 0.0).astype(BF16)
            placed[a] += dot(pick, sides)

    placed[...] = jnp.zeros((2, UTT, 2 * CH), F32)
    for w in range(2):
        for i in range(1, 4):
            wa(w, i).wait()
    for w in range(2):
        for i in range(1, 4):
            wb(w, i).start()

    @pl.loop(0, 8)
    def _(i):
        g = lax.rem(5 * i + 2, 8)
        for j in range(1, 4):
            routed(g * 4 + j).wait()

        @pl.when(g != 0)
        def _():
            routed(g * 4).wait()

        @pl.when(g == 0)
        def _():
            own_block.wait()

        place(g)

    def exchange(i):
        p = lax.rem(m + i, N_MP)
        return remote(exb.at[p], mg.at[m], ex_s.at[i], ex_r.at[i], d, p)

    for p in range(N_MP):
        exb[p] = placed[p % 2, :, (p // 2) * CH : (p // 2 + 1) * CH].astype(BF16)
    for i in range(1, N_MP):
        exchange(i).start()
    mg[m] = exb[m]

    for w in range(2):
        for i in range(1, 4):
            wb(w, i).wait()
        wc(w).start()
    own_rows.wait()

    def unpair(c):
        rows = pl.ds(pl.multiple_of(c * RC, RC), RC)
        for g in range(N_MP):
            s32[g] = xin[g, rows, :].astype(F32)
        for j in range(4):
            for g in range(N_MP):
                lanes = slice((j % 2) * C + g * CH, (j % 2) * C + (g + 1) * CH)
                pairs6[c, (j // 2) * FC : (j // 2 + 1) * FC, lanes] = s32[g, pl.ds(j, FC, stride=4), :].astype(BF16)

    def forward(c):
        pre = dot(pairs6[c], wts[0].reshape(2 * C, C))
        half = 0.5 * (1.0 + lax.erf(pre * inv_root_two))
        act = (pre * half).astype(BF16)
        slope6[c] = half + pre * jnp.exp(-0.5 * pre * pre) * inv_root_tau
        pairs7[c, :, 0:C] = act[:FC]
        pairs7[c, :, C : 2 * C] = act[FC:]
        pre = dot(pairs7[c], wts[1].reshape(2 * C, C))
        half = 0.5 * (1.0 + lax.erf(pre * inv_root_two))
        slope7[c] = half + pre * jnp.exp(-0.5 * pre * pre) * inv_root_tau

    @pl.loop(0, NCH)
    def _(c):
        for i in range(1, N_MP):
            feature(c, i).wait()
        unpair(c)

    for w in range(2):
        wc(w).wait()

    @pl.loop(0, NCH)
    def _(c):
        forward(c)

    for i in range(1, N_MP):
        exchange(i).wait()

    valid = lax.div(lens[m] - 400, 320) + 1

    def given(c, i):
        p = lax.rem(m + i, N_MP)
        return remote(
            gout.at[p, pl.ds(pl.multiple_of(c * RC, RC), RC), :],
            gf.at[pl.ds(pl.multiple_of(m * 4 * UTT + c * RC, RC), RC), :],
            go_s.at[c, i], go_r.at[c, i], d, p,
        )

    def own_given(c):
        return pltpu.make_async_copy(
            gout.at[m, pl.ds(pl.multiple_of(c * RC, RC), RC), :],
            gf.at[pl.ds(pl.multiple_of(m * 4 * UTT + c * RC, RC), RC), :],
            go_s.at[c, 0],
        )

    def backward(c):
        frames = pl.ds(pl.multiple_of(c * FC, FC), FC)
        live = iota((FC, CH), 0) + c * FC < valid
        for g in range(N_MP):
            lanes = slice(g * CH, (g + 1) * CH)
            coming = jnp.where(live, mg[g, frames, :].astype(F32), 0.0)
            delta7[c, :, lanes] = (coming * slope7[c, :, lanes]).astype(BF16)
        back = dot(delta7[c], wts[1].reshape(2 * C, C), ((1,), (1,)))
        delta6[c, 0:FC, :] = (back[:, :C] * slope6[c, 0:FC, :]).astype(BF16)
        delta6[c, FC : 2 * FC, :] = (back[:, C:] * slope6[c, FC : 2 * FC, :]).astype(BF16)
        back = dot(delta6[c], wts[0].reshape(2 * C, C), ((1,), (1,)))
        for j in range(4):
            for g in range(N_MP):
                s32[g, pl.ds(j, FC, stride=4), :] = back[
                    (j // 2) * FC : (j // 2 + 1) * FC, (j % 2) * C + g * CH : (j % 2) * C + (g + 1) * CH
                ]
        for g in range(N_MP):
            gout[g, pl.ds(pl.multiple_of(c * RC, RC), RC), :] = s32[g].astype(BF16)

    @pl.loop(0, NCH)
    def _(c):
        backward(c)
        for i in range(1, N_MP):
            given(c, i).start()
        own_given(c).start()

    def terms(w, b):
        pairs, deltas, count = ((pairs6, delta6, 2 * UTT), (pairs7, delta7, UTT))[w]
        left = pairs[:, :, pl.ds(pl.multiple_of(b * 256, 256), 256)].reshape(count, 256)
        right = deltas[...].reshape(count, C)
        gsum[w, b] = dot(left, right, ((0,), (0,))).reshape(4, 2, KR, C)

    def to_mate(w):
        return remote(core_out.at[w], core_in.at[w], rc_s.at[w], rc_r.at[w], dp_of(0, 0, 1), m)

    def ra(w, i):
        p = lax.rem((z, y)[w] + i, 4)
        return remote(
            part_out.at[w, p], part_in.at[w, i], ra_s.at[w, i], ra_r.at[w, i], (along_z, along_y)[w](i), m
        )

    def rb(w, i):
        p = lax.rem((y, z)[w] + i, 4)
        return remote(
            chip_out.at[w, p], chip_in.at[w, i], rb_s.at[w, i], rb_r.at[w, i], (along_y, along_z)[w](i), m
        )

    for w in (1, 0):

        @pl.loop(0, 4)
        def _(b):
            terms(w, b)
            core_out[w, b] = gsum[w, b, :, 1 - core].astype(BF16)

        to_mate(w).start()

    for w in (1, 0):
        to_mate(w).wait()

        @pl.loop(0, 4)
        def _(a):
            for b in range(4):
                zy = (a, b) if w == 0 else (b, a)
                total = gsum[w, zy[0], zy[1], core] + core_in[w, zy[0], zy[1]].astype(F32)
                part_out[w, a, b] = total.astype(BF16)

        for i in range(1, 4):
            ra(w, i).start()

    for w in (1, 0):
        for b in range(4):
            zy = (z, b) if w == 0 else (b, y)
            part[w, b] = gsum[w, zy[0], zy[1], core] + core_in[w, zy[0], zy[1]].astype(F32)
        for i in range(1, 4):
            ra(w, i).wait()
            part[w] += part_in[w, i].astype(F32)
        chip_out[w] = part[w].astype(BF16)
        for i in range(1, 4):
            rb(w, i).start()

    for w in (1, 0):
        share[w] = part[w, (y, z)[w]]
        for i in range(1, 4):
            rb(w, i).wait()
            share[w] += chip_in[w, i].astype(F32)
    for g in range(N_MP):
        x_out[g] = share[:, :, g * CH : (g + 1) * CH]

    def along(i):
        p = lax.rem(m + i, N_MP)
        return remote(x_out.at[p], x_in.at[i], rx_s.at[i], rx_r.at[i], d, p)

    for i in range(1, N_MP):
        along(i).start()
    total = x_out[m]
    for i in range(1, N_MP):
        along(i).wait()
        total = total + x_in[i]
    g6[...] = total[0]
    g7[...] = total[1]

    @pl.loop(0, NCH)
    def _(c):
        for i in range(1, N_MP):
            given(c, i).wait()
        own_given(c).wait()


def body(features, conv6_weight, conv7_weight, frame_grads, frame_dest, lengths):
    d = lax.axis_index("dp")
    own = lax.dynamic_slice_in_dim(frame_dest, d * FRM, FRM, 0).reshape(1, FRM)
    vmem, hbm = pl.BlockSpec(memory_space=pltpu.VMEM), pl.BlockSpec(memory_space=pl.ANY)
    dma = pltpu.SemaphoreType.DMA
    return pl.pallas_call(
        kernel,
        out_shape=(
            jax.ShapeDtypeStruct(features.shape, BF16),
            jax.ShapeDtypeStruct(conv6_weight.shape, F32),
            jax.ShapeDtypeStruct(conv7_weight.shape, F32),
        ),
        in_specs=[hbm, vmem, vmem, vmem, vmem, pl.BlockSpec(memory_space=pltpu.SMEM)],
        out_specs=(hbm, vmem, vmem),
        scratch_shapes=[
            pltpu.VMEM((N_MP, 4 * UTT, CH), BF16),
            pltpu.VMEM((2, 4, 4, 2, KR, C), BF16),
            pltpu.VMEM((8, FRM), jnp.int32),
            pltpu.VMEM((2, 2 * N_DP, 256), F32),
            pltpu.VMEM((FRM, 4 * CH), BF16),
            pltpu.VMEM((N_DP, BLK, CH), BF16),
            pltpu.VMEM((N_DP, BLK, CH), BF16),
            pltpu.VMEM((2, UTT, 2 * CH), F32),
            pltpu.VMEM((N_MP, UTT, CH), BF16),
            pltpu.VMEM((N_MP, UTT, CH), BF16),
            pltpu.VMEM((N_MP, RC, CH), F32),
            pltpu.VMEM((NCH, 2 * FC, 2 * C), BF16),
            pltpu.VMEM((NCH, FC, 2 * C), BF16),
            pltpu.VMEM((NCH, 2 * FC, C), F32),
            pltpu.VMEM((NCH, FC, C), F32),
            pltpu.VMEM((NCH, FC, C), BF16),
            pltpu.VMEM((NCH, 2 * FC, C), BF16),
            pltpu.VMEM((N_MP, 4 * UTT, CH), BF16),
            pltpu.VMEM((2, 4, 4, 2, KR, C), F32),
            pltpu.VMEM((2, 4, 4, KR, C), BF16),
            pltpu.VMEM((2, 4, 4, KR, C), BF16),
            pltpu.VMEM((2, 4, 4, KR, C), BF16),
            pltpu.VMEM((2, 4, 4, KR, C), BF16),
            pltpu.VMEM((2, 4, KR, C), F32),
            pltpu.VMEM((2, 4, KR, C), BF16),
            pltpu.VMEM((2, 4, KR, C), BF16),
            pltpu.VMEM((2, KR, C), F32),
            pltpu.VMEM((N_MP, 2, KR, CH), F32),
            pltpu.VMEM((N_MP, 2, KR, CH), F32),
            dma((N_MP, 2)), dma((N_MP, 2)), dma((2, 4)), dma((2, 4)), dma((2, 4)), dma((2, 4)), dma((2,)), dma((2,)),
            dma((1,)), dma((NCH, N_MP)), dma((NCH, N_MP)), dma((N_DP,)), dma((N_DP,)), dma((N_MP,)), dma((N_MP,)),
            dma((NCH, N_MP)), dma((NCH, N_MP)), dma((2,)), dma((2,)), dma((2, 4)), dma((2, 4)), dma((2, 4)), dma((2, 4)),
            dma((N_MP,)), dma((N_MP,)),
        ],
        compiler_params=pltpu.CompilerParams(
            collective_id=0, has_side_effects=True, vmem_limit_bytes=56 * 2**20,
            fuse_transposed_lhs_in_matmul=True,
        ),
        name="encoder_backward",
    )(features, conv6_weight, conv7_weight, frame_grads, own, lengths)


def solution(mesh):
    placed = (P("dp", "mp"), P("dp", "mp"), P("dp", "mp"), P("dp", "mp"), P(), P("dp"))
    return jax.shard_map(
        body,
        mesh=mesh,
        in_specs=placed,
        out_specs=(P("dp", "mp"), P("dp", "mp"), P("dp", "mp")),
        check_vma=False,
    )
```

time: 106 us -> 86.4 us (0.82)
  Pallas kernels: 99.1 us -> 79.2 us
    pallas_call x1, Pallas kernels: 99.1 us -> 79.2 us  [body(): pl.pallas_call(kernel, out_shape=(jax.ShapeDtypeStruct(features.shape, BF...]
where the time goes in v2:
time: 86.4 us; the launch traced here: 85.5 us
  Pallas kernels  79.2 us (92%)
  local copies, waits for them, and re-layouts  5.57 us (6%)
    pallas_call x1, Pallas kernels, body(): pl.pallas_call(kernel, out_shape=(jax.ShapeDtypeStruct(features.shape, BF...  79.2 us
    unnamed x7, local copies, waits for them, and re-layouts  4.27 us

profile of v2, /device:TPU:0, one launch (start us, length us, event | category | flops | bytes accessed | tf_op | source)
XLA Modules:
  0.0 85.5 jit_solution(15362763090116367420)
XLA Ops:
  0.6 1.3 %dynamic_slice.3 = s32[2048]{0:T(1024)} dynamic-slice(s32[65536]{0:T(1024)} %param.10, s32[]{:T(128)S(6)} %select_n.3), dynamic_slice_sizes={2048} | dynamic-slice | bytes 16388 | tf_op jit(solution)/shard_map/dynamic_slice | solution.py:421
  1.9 79.2 %encoder_backward.1 = (bf16[8192,128]{1,0:T(8,128)(2,1)}, f32[32,128]{1,0:T(8,128)}, f32[32,128]{1,0:T(8,128)}) custom-call(bf16[8192,128]{1,0:T(8,128)(2,1)} %feat.1, bf16[32,128]{1,0:T(8,128)(2,1)} %w6.1, bf16[32,128]{1,0:T(8,128)(2,1)} %w7.1, bf16[2048,128]{1,0:T(8,128)(2,1)} %grads.1, s32[1,2048]{1,0:T(1,128)} %bitcast.1, s32[4]{0:T(128)} %lens.1), custom_call_target="tpu_custom_call" | custom-call | tf_op jit(solution)/shard_map/encoder_backward/pallas_call | solution.py:424
  81.2 0.0 copy-start.1
  81.2 0.0 copy-start
  81.2 3.1 %copy.12 = bf16[8192,128]{1,0:T(8,128)(2,1)} copy(bf16[8192,128]{1,0:T(8,128)(2,1)} %get-tuple-element.6) | data formatting | bytes 4194304
  84.3 0.0 copy-done.1
  84.3 0.6 copy.13
  84.9 0.0 copy-done
  84.9 0.6 copy.14
Async XLA Ops:
  81.2 3.1 %copy-start.1 = (f32[32,128]{1,0:T(8,128)S(1)}, f32[32,128]{1,0:T(8,128)}, u32[]{:S(2)}) copy-start(f32[32,128]{1,0:T(8,128)} %get-tuple-element.7) | copy-start | bytes 49156
  81.2 3.7 %copy-start = (f32[32,128]{1,0:T(8,128)S(1)}, f32[32,128]{1,0:T(8,128)}, u32[]{:S(2)}) copy-start(f32[32,128]{1,0:T(8,128)} %get-tuple-element.8) | copy-start | bytes 49156

commit v3 on v2

--- a/solution.py
+++ b/solution.py
@@ -34,12 +34,12 @@
 
 
 def kernel(
-    feat, w6, w7, grads, dest, lens,
+    feat, w6, w7, grads_in, dest_in, lens_in,
     gf, g6, g7,
-    xin, wts, quad, meta, rhs, obox, arrived, placed, exb, mg,
+    grads, dest, lens, xin, wts, quad, meta, rhs, obox, arrived, placed, exb, mg,
     s32, pairs6, pairs7, slope6, slope7, delta7, delta6, gout,
     gsum, core_out, core_in, part_out, part_in, part, chip_out, chip_in, share, x_out, x_in,
-    wx_s, wx_r, wa_s, wa_r, wb_s, wb_r, wc_s, wc_r, own_sem, f_s, f_r, rt_s, rt_r, ex_s, ex_r,
+    wa_s, wa_r, wb_s, wb_r, wx_s, wx_r, wc_s, wc_r, own_sem, f_s, f_r, rt_s, rt_r, ex_s, ex_r,
     go_s, go_r, rc_s, rc_r, ra_s, ra_r, rb_s, rb_r, rx_s, rx_r,
 ):
     d, m = lax.axis_index("dp"), lax.axis_index("mp")
@@ -67,17 +67,44 @@
     )
     own_rows.start()
     cols = pl.ds(pl.multiple_of(m * CH, CH), CH)
-    wts[0, z, y, core, :, cols] = w6[...]
-    wts[1, z, y, core, :, cols] = w7[...]
+    local = [
+        pltpu.make_async_copy(dest_in.at[pl.ds(pl.multiple_of(d * FRM, FRM), FRM)], dest, own_sem.at[1]),
+        pltpu.make_async_copy(grads_in, grads, own_sem.at[2]),
+        pltpu.make_async_copy(w6, wts.at[0, z, y, core, :, cols], own_sem.at[3]),
+        pltpu.make_async_copy(w7, wts.at[1, z, y, core, :, cols], own_sem.at[4]),
+        pltpu.make_async_copy(lens_in, lens, own_sem.at[5]),
+    ]
+    for copy in local:
+        copy.start()
+    for copy in local:
+        copy.wait()
     pl.semaphore_wait(barrier, N_DP - 1 + N_MP - 1)
 
-    def wx(i, w):
+    def along_z(i):
+        return dp_of(i, 0, 0)
+
+    def along_y(i):
+        return dp_of(0, i, 0)
+
+    def wa(w, i):
         block = wts.at[w, z, y, core, :, cols]
-        return remote(block, block, wx_s.at[i, w], wx_r.at[i, w], d, lax.rem(m + i, N_MP))
-
-    for i in range(1, N_MP):
-        for w in range(2):
-            wx(i, w).start()
+        return remote(block, block, wa_s.at[w, i], wa_r.at[w, i], (along_z, along_y)[w](i), m)
+
+    def wb(w, i):
+        block = wts.at[0, :, y, core, :, cols] if w == 0 else wts.at[1, z, :, core, :, cols]
+        return remote(block, block, wb_s.at[w, i], wb_r.at[w, i], (along_y, along_z)[w](i), m)
+
+    def wx(w, i):
+        block = wts.at[w, :, :, core, :, cols]
+        return remote(block, block, wx_s.at[w, i], wx_r.at[w, i], d, lax.rem(m + i, N_MP))
+
+    def wc(w):
+        block = wts.at[w, :, :, core]
+        return remote(block, block, wc_s.at[w], wc_r.at[w], dp_of(0, 0, 1), m)
+
+    for w in range(2):
+        for i in range(1, 4):
+            wa(w, i).start()
 
     def feature(c, i):
         p = lax.rem(m + i, N_MP)
@@ -87,12 +114,12 @@
             f_s.at[c, i], f_r.at[c, i], d, p,
         )
 
-    for c in range(NCH):
+    for c in range(NCH // 2):
         for i in range(1, N_MP):
             feature(c, i).start()
 
     def number_slots():
-        target = dest[...]
+        target = dest[...].reshape(1, FRM)
         row = lax.bitwise_and(target, FRM - 1)
         shifted = lambda by, top: lax.bitwise_and(lax.shift_right_logical(target, by), top)
         owner = (
@@ -128,6 +155,12 @@
             meta[odd] = dot(digits, pick, ((1,), (1,)))
 
     number_slots()
+    for w in range(2):
+        for i in range(1, 4):
+            wa(w, i).wait()
+    for w in range(2):
+        for i in range(1, 4):
+            wb(w, i).start()
 
     def routed(k):
         return remote(
@@ -164,31 +197,15 @@
         def _():
             own_block.start()
 
-    for i in range(1, N_MP):
-        for w in range(2):
-            wx(i, w).wait()
-
-    def along_z(i):
-        return dp_of(i, 0, 0)
-
-    def along_y(i):
-        return dp_of(0, i, 0)
-
-    def wa(w, i):
-        block = wts.at[w, z, y, core]
-        return remote(block, block, wa_s.at[w, i], wa_r.at[w, i], (along_z, along_y)[w](i), m)
-
-    def wb(w, i):
-        block = wts.at[0, :, y, core] if w == 0 else wts.at[1, z, :, core]
-        return remote(block, block, wb_s.at[w, i], wb_r.at[w, i], (along_y, along_z)[w](i), m)
-
-    def wc(w):
-        block = wts.at[w, :, :, core]
-        return remote(block, block, wc_s.at[w], wc_r.at[w], dp_of(0, 0, 1), m)
-
-    for w in range(2):
-        for i in range(1, 4):
-            wa(w, i).start()
+    for w in range(2):
+        for i in range(1, 4):
+            wb(w, i).wait()
+    for w in range(2):
+        for i in range(1, 4):
+            wx(w, i).start()
+    for c in range(NCH // 2, NCH):
+        for i in range(1, N_MP):
+            feature(c, i).start()
 
     def place(g):
         first, second = [], []
@@ -216,12 +233,6 @@
             placed[a] += dot(pick, sides)
 
     placed[...] = jnp.zeros((2, UTT, 2 * CH), F32)
-    for w in range(2):
-        for i in range(1, 4):
-            wa(w, i).wait()
-    for w in range(2):
-        for i in range(1, 4):
-            wb(w, i).start()
 
     @pl.loop(0, 8)
     def _(i):
@@ -251,7 +262,7 @@
 
     for w in range(2):
         for i in range(1, 4):
-            wb(w, i).wait()
+            wx(w, i).wait()
         wc(w).start()
     own_rows.wait()
 
@@ -417,8 +428,6 @@
 
 
 def body(features, conv6_weight, conv7_weight, frame_grads, frame_dest, lengths):
-    d = lax.axis_index("dp")
-    own = lax.dynamic_slice_in_dim(frame_dest, d * FRM, FRM, 0).reshape(1, FRM)
     vmem, hbm = pl.BlockSpec(memory_space=pltpu.VMEM), pl.BlockSpec(memory_space=pl.ANY)
     dma = pltpu.SemaphoreType.DMA
     return pl.pallas_call(
@@ -428,9 +437,12 @@
             jax.ShapeDtypeStruct(conv6_weight.shape, F32),
             jax.ShapeDtypeStruct(conv7_weight.shape, F32),
         ),
-        in_specs=[hbm, vmem, vmem, vmem, vmem, pl.BlockSpec(memory_space=pltpu.SMEM)],
+        in_specs=[hbm] * 6,
         out_specs=(hbm, vmem, vmem),
         scratch_shapes=[
+            pltpu.VMEM((FRM, CH), BF16),
+            pltpu.VMEM((FRM,), jnp.int32),
+            pltpu.SMEM((N_MP,), jnp.int32),
             pltpu.VMEM((N_MP, 4 * UTT, CH), BF16),
             pltpu.VMEM((2, 4, 4, 2, KR, C), BF16),
             pltpu.VMEM((8, FRM), jnp.int32),
@@ -460,8 +472,8 @@
             pltpu.VMEM((2, KR, C), F32),
             pltpu.VMEM((N_MP, 2, KR, CH), F32),
             pltpu.VMEM((N_MP, 2, KR, CH), F32),
-            dma((N_MP, 2)), dma((N_MP, 2)), dma((2, 4)), dma((2, 4)), dma((2, 4)), dma((2, 4)), dma((2,)), dma((2,)),
-            dma((1,)), dma((NCH, N_MP)), dma((NCH, N_MP)), dma((N_DP,)), dma((N_DP,)), dma((N_MP,)), dma((N_MP,)),
+            dma((2, 4)), dma((2, 4)), dma((2, 4)), dma((2, 4)), dma((2, 4)), dma((2, 4)), dma((2,)), dma((2,)),
+            dma((6,)), dma((NCH, N_MP)), dma((NCH, N_MP)), dma((N_DP,)), dma((N_DP,)), dma((N_MP,)), dma((N_MP,)),
             dma((NCH, N_MP)), dma((NCH, N_MP)), dma((2,)), dma((2,)), dma((2, 4)), dma((2, 4)), dma((2, 4)), dma((2, 4)),
             dma((N_MP,)), dma((N_MP,)),
         ],
@@ -470,7 +482,7 @@
             fuse_transposed_lhs_in_matmul=True,
         ),
         name="encoder_backward",
-    )(features, conv6_weight, conv7_weight, frame_grads, own, lengths)
+    )(features, conv6_weight, conv7_weight, frame_grads, frame_dest, lengths)
 
 
 def solution(mesh):

time: 86.4 us -> 86 us (level)
  local copies, waits for them, and re-layouts: 5.57 us -> 4.27 us
  Pallas kernels: 79.2 us -> 80.3 us
    dynamic_slice x1 -> x0, local copies, waits for them, and re-layouts: 1.3 us -> none  [body(): own = lax.dynamic_slice_in_dim(frame_dest, d * FRM, FRM, 0).reshape(1, FRM)]
    pallas_call x1, Pallas kernels: 79.2 us -> 80.3 us  [body(): pl.pallas_call(kernel, out_shape=(jax.ShapeDtypeStruct(features.shape, BF...]
where the time goes in v3:
time: 86 us; the launch traced here: 85.3 us
  Pallas kernels  80.3 us (93%)
  local copies, waits for them, and re-layouts  4.27 us (5%)
    pallas_call x1, Pallas kernels, body(): pl.pallas_call(kernel, out_shape=(jax.ShapeDtypeStruct(features.shape, BF...  80.3 us
    unnamed x7, local copies, waits for them, and re-layouts  4.27 us

profile of v3, /device:TPU:0, one launch (start us, length us, event | category | flops | bytes accessed | tf_op | source)
XLA Modules:
  0.0 85.3 jit_solution(10318046058771123397)
XLA Ops:
  0.6 80.3 %encoder_backward.1 = (bf16[8192,128]{1,0:T(8,128)(2,1)}, f32[32,128]{1,0:T(8,128)}, f32[32,128]{1,0:T(8,128)}) custom-call(bf16[8192,128]{1,0:T(8,128)(2,1)} %feat.1, bf16[32,128]{1,0:T(8,128)(2,1)} %w6.1, bf16[32,128]{1,0:T(8,128)(2,1)} %w7.1, bf16[2048,128]{1,0:T(8,128)(2,1)} %grads_in.1, s32[65536]{0:T(1024)} %dest_in.1, s32[4]{0:T(128)} %lens_in.1), custom_call_target="tpu_custom_call" | custom-call | tf_op jit(solution)/shard_map/encoder_backward/pallas_call | solution.py:433
  81.0 0.0 copy-start.1
  81.0 0.0 copy-start
  81.0 3.1 %copy.12 = bf16[8192,128]{1,0:T(8,128)(2,1)} copy(bf16[8192,128]{1,0:T(8,128)(2,1)} %get-tuple-element.6) | data formatting | bytes 4194304
  84.1 0.0 copy-done.1
  84.1 0.6 copy.13
  84.7 0.0 copy-done
  84.7 0.6 copy.14
Async XLA Ops:
  81.0 3.1 %copy-start.1 = (f32[32,128]{1,0:T(8,128)S(1)}, f32[32,128]{1,0:T(8,128)}, u32[]{:S(2)}) copy-start(f32[32,128]{1,0:T(8,128)} %get-tuple-element.7) | copy-start | bytes 49156
  81.0 3.7 %copy-start = (f32[32,128]{1,0:T(8,128)S(1)}, f32[32,128]{1,0:T(8,128)}, u32[]{:S(2)}) copy-start(f32[32,128]{1,0:T(8,128)} %get-tuple-element.8) | copy-start | bytes 49156

commit v4 on v3

--- a/solution.py
+++ b/solution.py
@@ -39,7 +39,7 @@
     grads, dest, lens, xin, wts, quad, meta, rhs, obox, arrived, placed, exb, mg,
     s32, pairs6, pairs7, slope6, slope7, delta7, delta6, gout,
     gsum, core_out, core_in, part_out, part_in, part, chip_out, chip_in, share, x_out, x_in,
-    wa_s, wa_r, wb_s, wb_r, wx_s, wx_r, wc_s, wc_r, own_sem, f_s, f_r, rt_s, rt_r, ex_s, ex_r,
+    va_s, va_r, vb_s, vb_r, vx_s, vx_r, ux_s, ux_r, ua_s, ua_r, ub_s, ub_r, wc_s, wc_r, own_sem, f_s, f_r, rt_s, rt_r, ex_s, ex_r,
     go_s, go_r, rc_s, rc_r, ra_s, ra_r, rb_s, rb_r, rx_s, rx_r,
 ):
     d, m = lax.axis_index("dp"), lax.axis_index("mp")
@@ -86,25 +86,38 @@
     def along_y(i):
         return dp_of(0, i, 0)
 
-    def wa(w, i):
-        block = wts.at[w, z, y, core, :, cols]
-        return remote(block, block, wa_s.at[w, i], wa_r.at[w, i], (along_z, along_y)[w](i), m)
-
-    def wb(w, i):
-        block = wts.at[0, :, y, core, :, cols] if w == 0 else wts.at[1, z, :, core, :, cols]
-        return remote(block, block, wb_s.at[w, i], wb_r.at[w, i], (along_y, along_z)[w](i), m)
-
-    def wx(w, i):
-        block = wts.at[w, :, :, core, :, cols]
-        return remote(block, block, wx_s.at[w, i], wx_r.at[w, i], d, lax.rem(m + i, N_MP))
+    def va(i):
+        block = wts.at[1, z, y, core, :, cols]
+        return remote(block, block, va_s.at[i], va_r.at[i], along_y(i), m)
+
+    def vb(i):
+        block = wts.at[1, z, :, core, :, cols]
+        return remote(block, block, vb_s.at[i], vb_r.at[i], along_z(i), m)
+
+    def vx(i):
+        block = wts.at[1, :, :, core, :, cols]
+        return remote(block, block, vx_s.at[i], vx_r.at[i], d, lax.rem(m + i, N_MP))
+
+    def ux(i):
+        block = wts.at[0, z, y, core, :, cols]
+        return remote(block, block, ux_s.at[i], ux_r.at[i], d, lax.rem(m + i, N_MP))
+
+    def ua(h, i):
+        block = wts.at[0, z, y, core, :, pl.ds(h * 256, 256)]
+        return remote(block, block, ua_s.at[h, i], ua_r.at[h, i], (along_z, along_y)[h](i), m)
+
+    def ub(h, i):
+        half = pl.ds(h * 256, 256)
+        block = wts.at[0, :, y, core, :, half] if h == 0 else wts.at[0, z, :, core, :, half]
+        return remote(block, block, ub_s.at[h, i], ub_r.at[h, i], (along_y, along_z)[h](i), m)
 
     def wc(w):
         block = wts.at[w, :, :, core]
         return remote(block, block, wc_s.at[w], wc_r.at[w], dp_of(0, 0, 1), m)
 
-    for w in range(2):
-        for i in range(1, 4):
-            wa(w, i).start()
+    for i in range(1, 4):
+        ux(i).start()
+        va(i).start()
 
     def feature(c, i):
         p = lax.rem(m + i, N_MP)
@@ -155,12 +168,13 @@
             meta[odd] = dot(digits, pick, ((1,), (1,)))
 
     number_slots()
-    for w in range(2):
-        for i in range(1, 4):
-            wa(w, i).wait()
-    for w in range(2):
-        for i in range(1, 4):
-            wb(w, i).start()
+    for i in range(1, 4):
+        va(i).wait()
+        ux(i).wait()
+    for i in range(1, 4):
+        vb(i).start()
+        ua(0, i).start()
+        ua(1, i).start()
 
     def routed(k):
         return remote(
@@ -197,12 +211,14 @@
         def _():
             own_block.start()
 
-    for w in range(2):
-        for i in range(1, 4):
-            wb(w, i).wait()
-    for w in range(2):
-        for i in range(1, 4):
-            wx(w, i).start()
+    for i in range(1, 4):
+        vb(i).wait()
+        ua(0, i).wait()
+        ua(1, i).wait()
+    for i in range(1, 4):
+        vx(i).start()
+        ub(0, i).start()
+        ub(1, i).start()
     for c in range(NCH // 2, NCH):
         for i in range(1, N_MP):
             feature(c, i).start()
@@ -260,10 +276,13 @@
         exchange(i).start()
     mg[m] = exb[m]
 
-    for w in range(2):
-        for i in range(1, 4):
-            wx(w, i).wait()
-        wc(w).start()
+    for i in range(1, 4):
+        ub(0, i).wait()
+        ub(1, i).wait()
+    wc(0).start()
+    for i in range(1, 4):
+        vx(i).wait()
+    wc(1).start()
     own_rows.wait()
 
     def unpair(c):
@@ -286,17 +305,17 @@
         half = 0.5 * (1.0 + lax.erf(pre * inv_root_two))
         slope7[c] = half + pre * jnp.exp(-0.5 * pre * pre) * inv_root_tau
 
-    @pl.loop(0, NCH)
-    def _(c):
+    for c in range(2):
         for i in range(1, N_MP):
             feature(c, i).wait()
         unpair(c)
-
     for w in range(2):
         wc(w).wait()
-
-    @pl.loop(0, NCH)
-    def _(c):
+    for c in range(NCH):
+        if c >= 2:
+            for i in range(1, N_MP):
+                feature(c, i).wait()
+            unpair(c)
         forward(c)
 
     for i in range(1, N_MP):
@@ -427,10 +446,21 @@
         own_given(c).wait()
 
 
+def hand_over(gf, g6, g7, gf_out, g6_out, g7_out, sem):
+    copies = [pltpu.make_async_copy(g6, g6_out, sem.at[N_MP]), pltpu.make_async_copy(g7, g7_out, sem.at[N_MP + 1])]
+    for p in range(N_MP):
+        rows = pl.ds(p * 4 * UTT, 4 * UTT)
+        copies.append(pltpu.make_async_copy(gf.at[rows], gf_out.at[rows], sem.at[p]))
+    for copy in copies:
+        copy.start()
+    for copy in copies:
+        copy.wait()
+
+
 def body(features, conv6_weight, conv7_weight, frame_grads, frame_dest, lengths):
     vmem, hbm = pl.BlockSpec(memory_space=pltpu.VMEM), pl.BlockSpec(memory_space=pl.ANY)
     dma = pltpu.SemaphoreType.DMA
-    return pl.pallas_call(
+    results = pl.pallas_call(
         kernel,
         out_shape=(
             jax.ShapeDtypeStruct(features.shape, BF16),
@@ -472,7 +502,8 @@
             pltpu.VMEM((2, KR, C), F32),
             pltpu.VMEM((N_MP, 2, KR, CH), F32),
             pltpu.VMEM((N_MP, 2, KR, CH), F32),
-            dma((2, 4)), dma((2, 4)), dma((2, 4)), dma((2, 4)), dma((2, 4)), dma((2, 4)), dma((2,)), dma((2,)),
+            dma((4,)), dma((4,)), dma((4,)), dma((4,)), dma((4,)), dma((4,)), dma((4,)), dma((4,)),
+            dma((2, 4)), dma((2, 4)), dma((2, 4)), dma((2, 4)), dma((2,)), dma((2,)),
             dma((6,)), dma((NCH, N_MP)), dma((NCH, N_MP)), dma((N_DP,)), dma((N_DP,)), dma((N_MP,)), dma((N_MP,)),
             dma((NCH, N_MP)), dma((NCH, N_MP)), dma((2,)), dma((2,)), dma((2, 4)), dma((2, 4)), dma((2, 4)), dma((2, 4)),
             dma((N_MP,)), dma((N_MP,)),
@@ -483,6 +514,14 @@
         ),
         name="encoder_backward",
     )(features, conv6_weight, conv7_weight, frame_grads, frame_dest, lengths)
+    return pl.pallas_call(
+        hand_over,
+        out_shape=tuple(jax.ShapeDtypeStruct(r.shape, r.dtype) for r in results),
+        in_specs=[hbm] * 3,
+        out_specs=(hbm,) * 3,
+        scratch_shapes=[dma((N_MP + 2,))],
+        name="hand_over",
+    )(*results)
 
 
 def solution(mesh):

time: 86 us -> 143 us (1.66)
  Pallas kernels: 80.3 us -> 142 us
  local copies, waits for them, and re-layouts: 4.27 us -> 0 us
    pallas_call x0 -> x1, Pallas kernels: none -> 65.7 us  [body(): pl.pallas_call(hand_over, out_shape=tuple((jax.ShapeDtypeStruct(r.shape,...]
    unnamed x7 -> x0, local copies, waits for them, and re-layouts: 4.27 us -> none
    pallas_call x1, Pallas kernels: 80.3 us -> 76.3 us  [body(): pl.pallas_call(kernel, out_shape=(jax.ShapeDtypeStruct(features.shape, BF...]
where the time goes in v4:
time: 143 us
  Pallas kernels  142 us (99%)
    pallas_call x1, Pallas kernels, body(): pl.pallas_call(kernel, out_shape=(jax.ShapeDtypeStruct(features.shape, BF...  76.3 us
    pallas_call x1, Pallas kernels, body(): pl.pallas_call(hand_over, out_shape=tuple((jax.ShapeDtypeStruct(r.shape,...  65.7 us

profile of v4, /device:TPU:0, one launch (start us, length us, event | category | flops | bytes accessed | tf_op | source)
XLA Modules:
  0.0 142.6 jit_solution(891234205781196637)
XLA Ops:
  0.6 76.3 %encoder_backward.1 = (bf16[8192,128]{1,0:T(8,128)(2,1)}, f32[32,128]{1,0:T(8,128)}, f32[32,128]{1,0:T(8,128)}) custom-call(bf16[8192,128]{1,0:T(8,128)(2,1)} %feat.1, bf16[32,128]{1,0:T(8,128)(2,1)} %w6.1, bf16[32,128]{1,0:T(8,128)(2,1)} %w7.1, bf16[2048,128]{1,0:T(8,128)(2,1)} %grads_in.1, s32[65536]{0:T(1024)} %dest_in.1, s32[4]{0:T(128)} %lens_in.1), custom_call_target="tpu_custom_call" | custom-call | tf_op jit(solution)/shard_map/encoder_backward/pallas_call | solution.py:463
  76.9 65.7 %hand_over.1 = (bf16[8192,128]{1,0:T(8,128)(2,1)}, f32[32,128]{1,0:T(8,128)}, f32[32,128]{1,0:T(8,128)}) custom-call(bf16[8192,128]{1,0:T(8,128)(2,1)} %get-tuple-element.6.gf, f32[32,128]{1,0:T(8,128)} %get-tuple-element.7.g6, f32[32,128]{1,0:T(8,128)} %get-tuple-element.8.g7), custom_call_target="tpu_custom_call" | custom-call | tf_op jit(solution)/shard_map/hand_over/pallas_call | solution.py:517

commit v5 on v4

--- a/solution.py
+++ b/solution.py
@@ -15,6 +15,7 @@
 FC = 128
 NCH = UTT // FC
 RC = 4 * FC
+PARTS = 8
 META = 16
 BLK = CAP + META
 KR = 32
@@ -446,14 +447,19 @@
         own_given(c).wait()
 
 
-def hand_over(gf, g6, g7, gf_out, g6_out, g7_out, sem):
-    copies = [pltpu.make_async_copy(g6, g6_out, sem.at[N_MP]), pltpu.make_async_copy(g7, g7_out, sem.at[N_MP + 1])]
-    for p in range(N_MP):
-        rows = pl.ds(p * 4 * UTT, 4 * UTT)
-        copies.append(pltpu.make_async_copy(gf.at[rows], gf_out.at[rows], sem.at[p]))
-    for copy in copies:
+def hand_over(gf, g6, g7, gf_out, g6_out, g7_out, held, held6, held7, sem_in, sem_out):
+    steps = [(g6, held6, g6_out), (g7, held7, g7_out)]
+    for p in range(PARTS):
+        rows = pl.ds(p * (16 * UTT // PARTS), 16 * UTT // PARTS)
+        steps.append((gf.at[rows], held.at[rows], gf_out.at[rows]))
+    come = [pltpu.make_async_copy(a, b, sem_in.at[n]) for n, (a, b, _) in enumerate(steps)]
+    go = [pltpu.make_async_copy(b, c, sem_out.at[n]) for n, (_, b, c) in enumerate(steps)]
+    for copy in come:
         copy.start()
-    for copy in copies:
+    for here, there in zip(come, go):
+        here.wait()
+        there.start()
+    for copy in go:
         copy.wait()
 
 
@@ -519,7 +525,10 @@
         out_shape=tuple(jax.ShapeDtypeStruct(r.shape, r.dtype) for r in results),
         in_specs=[hbm] * 3,
         out_specs=(hbm,) * 3,
-        scratch_shapes=[dma((N_MP + 2,))],
+        scratch_shapes=[
+            pltpu.VMEM((16 * UTT, CH), BF16), pltpu.VMEM((KR, CH), F32), pltpu.VMEM((KR, CH), F32),
+            dma((PARTS + 2,)), dma((PARTS + 2,)),
+        ],
         name="hand_over",
     )(*results)
 

time: 143 us -> 79.8 us (0.56)
  Pallas kernels: 142 us -> 78.8 us
    pallas_call x1, Pallas kernels: 65.7 us -> 2.46 us  [body(): pl.pallas_call(hand_over, out_shape=tuple((jax.ShapeDtypeStruct(r.shape,...]
where the time goes in v5:
time: 79.8 us; the launch traced here: 79.4 us
  Pallas kernels  78.8 us (99%)
    pallas_call x1, Pallas kernels, body(): pl.pallas_call(kernel, out_shape=(jax.ShapeDtypeStruct(features.shape, BF...  76.3 us
    pallas_call x1, Pallas kernels, body(): pl.pallas_call(hand_over, out_shape=tuple((jax.ShapeDtypeStruct(r.shape,...  2.46 us

profile of v5, /device:TPU:0, one launch (start us, length us, event | category | flops | bytes accessed | tf_op | source)
XLA Modules:
  0.0 79.4 jit_solution(6845347087685189269)
XLA Ops:
  0.6 76.3 %encoder_backward.1 = (bf16[8192,128]{1,0:T(8,128)(2,1)}, f32[32,128]{1,0:T(8,128)}, f32[32,128]{1,0:T(8,128)}) custom-call(bf16[8192,128]{1,0:T(8,128)(2,1)} %feat.1, bf16[32,128]{1,0:T(8,128)(2,1)} %w6.1, bf16[32,128]{1,0:T(8,128)(2,1)} %w7.1, bf16[2048,128]{1,0:T(8,128)(2,1)} %grads_in.1, s32[65536]{0:T(1024)} %dest_in.1, s32[4]{0:T(128)} %lens_in.1), custom_call_target="tpu_custom_call" | custom-call | tf_op jit(solution)/shard_map/encoder_backward/pallas_call | solution.py:469
  76.9 2.5 %hand_over.1 = (bf16[8192,128]{1,0:T(8,128)(2,1)}, f32[32,128]{1,0:T(8,128)}, f32[32,128]{1,0:T(8,128)}) custom-call(bf16[8192,128]{1,0:T(8,128)(2,1)} %get-tuple-element.6.gf, f32[32,128]{1,0:T(8,128)} %get-tuple-element.7.g6, f32[32,128]{1,0:T(8,128)} %get-tuple-element.8.g7), custom_call_target="tpu_custom_call" | custom-call | tf_op jit(solution)/shard_map/hand_over/pallas_call | solution.py:523

commit v6 on v5

--- a/solution.py
+++ b/solution.py
@@ -218,8 +218,6 @@
         ua(1, i).wait()
     for i in range(1, 4):
         vx(i).start()
-        ub(0, i).start()
-        ub(1, i).start()
     for c in range(NCH // 2, NCH):
         for i in range(1, N_MP):
             feature(c, i).start()
@@ -267,6 +265,12 @@
 
         place(g)
 
+        @pl.when(i == 3)
+        def _():
+            for n in range(1, 4):
+                ub(0, n).start()
+                ub(1, n).start()
+
     def exchange(i):
         p = lax.rem(m + i, N_MP)
         return remote(exb.at[p], mg.at[m], ex_s.at[i], ex_r.at[i], d, p)
@@ -306,17 +310,13 @@
         half = 0.5 * (1.0 + lax.erf(pre * inv_root_two))
         slope7[c] = half + pre * jnp.exp(-0.5 * pre * pre) * inv_root_tau
 
-    for c in range(2):
+    for c in range(NCH):
         for i in range(1, N_MP):
             feature(c, i).wait()
         unpair(c)
     for w in range(2):
         wc(w).wait()
     for c in range(NCH):
-        if c >= 2:
-            for i in range(1, N_MP):
-                feature(c, i).wait()
-            unpair(c)
         forward(c)
 
     for i in range(1, N_MP):

time: 79.8 us -> 77.7 us (0.974)
  Pallas kernels: 78.8 us -> 76.9 us
    pallas_call x1, Pallas kernels: 76.3 us -> 74.4 us  [body(): pl.pallas_call(kernel, out_shape=(jax.ShapeDtypeStruct(features.shape, BF...]
where the time goes in v6:
time: 77.7 us; the launch traced here: 77.5 us
  Pallas kernels  76.9 us (99%)
    pallas_call x1, Pallas kernels, body(): pl.pallas_call(kernel, out_shape=(jax.ShapeDtypeStruct(features.shape, BF...  74.4 us
    pallas_call x1, Pallas kernels, body(): pl.pallas_call(hand_over, out_shape=tuple((jax.ShapeDtypeStruct(r.shape,...  2.46 us

profile of v6, /device:TPU:0, one launch (start us, length us, event | category | flops | bytes accessed | tf_op | source)
XLA Modules:
  0.0 77.5 jit_solution(14474741711578888059)
XLA Ops:
  0.6 74.4 %encoder_backward.1 = (bf16[8192,128]{1,0:T(8,128)(2,1)}, f32[32,128]{1,0:T(8,128)}, f32[32,128]{1,0:T(8,128)}) custom-call(bf16[8192,128]{1,0:T(8,128)(2,1)} %feat.1, bf16[32,128]{1,0:T(8,128)(2,1)} %w6.1, bf16[32,128]{1,0:T(8,128)(2,1)} %w7.1, bf16[2048,128]{1,0:T(8,128)(2,1)} %grads_in.1, s32[65536]{0:T(1024)} %dest_in.1, s32[4]{0:T(128)} %lens_in.1), custom_call_target="tpu_custom_call" | custom-call | tf_op jit(solution)/shard_map/encoder_backward/pallas_call | solution.py:469
  75.0 2.5 %hand_over.1 = (bf16[8192,128]{1,0:T(8,128)(2,1)}, f32[32,128]{1,0:T(8,128)}, f32[32,128]{1,0:T(8,128)}) custom-call(bf16[8192,128]{1,0:T(8,128)(2,1)} %get-tuple-element.6.gf, f32[32,128]{1,0:T(8,128)} %get-tuple-element.7.g6, f32[32,128]{1,0:T(8,128)} %get-tuple-element.8.g7), custom_call_target="tpu_custom_call" | custom-call | tf_op jit(solution)/shard_map/hand_over/pallas_call | solution.py:523

commit v7 on v6

--- a/solution.py
+++ b/solution.py
@@ -16,8 +16,6 @@
 NCH = UTT // FC
 RC = 4 * FC
 PARTS = 8
-META = 16
-BLK = CAP + META
 KR = 32
 
 inv_root_two = 0.7071067811865476
@@ -37,10 +35,10 @@
 def kernel(
     feat, w6, w7, grads_in, dest_in, lens_in,
     gf, g6, g7,
-    grads, dest, lens, xin, wts, quad, meta, rhs, obox, arrived, placed, exb, mg,
+    grads, dest, lens, xin, wts, quad, meta, rhs, obox, arrived, rows_out, rows_in, placed, exb, mg,
     s32, pairs6, pairs7, slope6, slope7, delta7, delta6, gout,
     gsum, core_out, core_in, part_out, part_in, part, chip_out, chip_in, share, x_out, x_in,
-    va_s, va_r, vb_s, vb_r, vx_s, vx_r, ux_s, ux_r, ua_s, ua_r, ub_s, ub_r, wc_s, wc_r, own_sem, f_s, f_r, rt_s, rt_r, ex_s, ex_r,
+    va_s, va_r, vb_s, vb_r, vx_s, vx_r, ux_s, ux_r, ua_s, ua_r, ub_s, ub_r, wc_s, wc_r, own_sem, f_s, f_r, rt_s, rt_r, rn_s, rn_r, ex_s, ex_r,
     go_s, go_r, rc_s, rc_r, ra_s, ra_r, rb_s, rb_r, rx_s, rx_r,
 ):
     d, m = lax.axis_index("dp"), lax.axis_index("mp")
@@ -183,33 +181,42 @@
             dp_of(lax.div(k, 8), lax.rem(lax.div(k, 2), 4), lax.rem(k, 2)), m,
         )
 
+    def numbers(k):
+        return remote(
+            rows_out.at[k], rows_in.at[k], rn_s.at[k], rn_r.at[k],
+            dp_of(lax.div(k, 8), lax.rem(lax.div(k, 2), 4), lax.rem(k, 2)), m,
+        )
+
+    own_numbers = pltpu.make_async_copy(rows_out.at[0], rows_in.at[0], rn_r.at[0])
     own_block = pltpu.make_async_copy(obox.at[0], arrived.at[0], rt_r.at[0])
 
     def pack(g):
         pick = jnp.where(iota((CAP, FRM), 0) == quad[pl.ds(g, 1), :], 1.0, 0.0).astype(BF16)
         both = dot(pick, rhs[...])
-        line = iota((META, 128), 0)
         for j in range(4):
             k = g * 4 + j
-            obox[k, 0:CAP, :] = both[:, j * CH : (j + 1) * CH].astype(BF16)
+            obox[k] = both[:, j * CH : (j + 1) * CH].astype(BF16)
             high, low = meta[j % 2, pl.ds(k, 1), :], meta[j % 2, pl.ds(k + N_DP, 1), :]
-            tile = jnp.where(line == 0, high[:, :128], jnp.where(line == 1, high[:, 128:], 0.0))
-            tile = jnp.where(line == 2, low[:, :128], jnp.where(line == 3, low[:, 128:], tile))
-            obox[k, CAP:BLK, :] = tile.astype(BF16)
+            rows = high * 256.0 + low
+            rows_out[k, 0:1, :] = rows[:, :128]
+            rows_out[k, 1:2, :] = rows[:, 128:]
 
     @pl.loop(0, 8)
     def _(i):
         g = lax.rem(5 * i + 2, 8)
         pack(g)
         for j in range(1, 4):
+            numbers(g * 4 + j).start()
             routed(g * 4 + j).start()
 
         @pl.when(g != 0)
         def _():
+            numbers(g * 4).start()
             routed(g * 4).start()
 
         @pl.when(g == 0)
         def _():
+            own_numbers.start()
             own_block.start()
 
     for i in range(1, 4):
@@ -225,9 +232,8 @@
     def place(g):
         first, second = [], []
         for i in range(4):
-            digits = arrived[g * 4 + i, CAP:BLK, :].astype(F32)
-            first.append(digits[0:1] * 256.0 + digits[2:3])
-            second.append(digits[1:2] * 256.0 + digits[3:4])
+            first.append(rows_in[g * 4 + i, 0:1, :])
+            second.append(rows_in[g * 4 + i, 1:2, :])
         left = iota((1, 128), 1) < 64
         at = jnp.concatenate(
             [
@@ -240,7 +246,7 @@
         within = lax.bitwise_and(at, 1023)
         top = jnp.where(iota((8, 4 * CAP), 0) == 0, half, 0).astype(F32).astype(BF16)
         later = dot(top, jnp.ones((8, CH), BF16), ((0,), (0,))).astype(BF16)
-        block = arrived[pl.ds(g * 4, 4), 0:CAP, :].reshape(4 * CAP, CH)
+        block = arrived[pl.ds(g * 4, 4)].reshape(4 * CAP, CH)
         second_half = block * later
         sides = jnp.concatenate([block - second_half, second_half], axis=1)
         for a in range(2):
@@ -253,14 +259,17 @@
     def _(i):
         g = lax.rem(5 * i + 2, 8)
         for j in range(1, 4):
+            numbers(g * 4 + j).wait()
             routed(g * 4 + j).wait()
 
         @pl.when(g != 0)
         def _():
+            numbers(g * 4).wait()
             routed(g * 4).wait()
 
         @pl.when(g == 0)
         def _():
+            own_numbers.wait()
             own_block.wait()
 
         place(g)
@@ -484,8 +493,10 @@
             pltpu.VMEM((8, FRM), jnp.int32),
             pltpu.VMEM((2, 2 * N_DP, 256), F32),
             pltpu.VMEM((FRM, 4 * CH), BF16),
-            pltpu.VMEM((N_DP, BLK, CH), BF16),
-            pltpu.VMEM((N_DP, BLK, CH), BF16),
+            pltpu.VMEM((N_DP, CAP, CH), BF16),
+            pltpu.VMEM((N_DP, CAP, CH), BF16),
+            pltpu.VMEM((N_DP, 2, 128), F32),
+            pltpu.VMEM((N_DP, 2, 128), F32),
             pltpu.VMEM((2, UTT, 2 * CH), F32),
             pltpu.VMEM((N_MP, UTT, CH), BF16),
             pltpu.VMEM((N_MP, UTT, CH), BF16),
@@ -510,7 +521,7 @@
             pltpu.VMEM((N_MP, 2, KR, CH), F32),
             dma((4,)), dma((4,)), dma((4,)), dma((4,)), dma((4,)), dma((4,)), dma((4,)), dma((4,)),
             dma((2, 4)), dma((2, 4)), dma((2, 4)), dma((2, 4)), dma((2,)), dma((2,)),
-            dma((6,)), dma((NCH, N_MP)), dma((NCH, N_MP)), dma((N_DP,)), dma((N_DP,)), dma((N_MP,)), dma((N_MP,)),
+            dma((6,)), dma((NCH, N_MP)), dma((NCH, N_MP)), dma((N_DP,)), dma((N_DP,)), dma((N_DP,)), dma((N_DP,)), dma((N_MP,)), dma((N_MP,)),
             dma((NCH, N_MP)), dma((NCH, N_MP)), dma((2,)), dma((2,)), dma((2, 4)), dma((2, 4)), dma((2, 4)), dma((2, 4)),
             dma((N_MP,)), dma((N_MP,)),
         ],

time: 77.7 us -> 78.1 us (level)
  no operation moved by 1% of the time
where the time goes in v7:
time: 78.1 us; the launch traced here: 77.9 us
  Pallas kernels  77.3 us (99%)
    pallas_call x1, Pallas kernels, body(): pl.pallas_call(kernel, out_shape=(jax.ShapeDtypeStruct(features.shape, BF...  74.8 us
    pallas_call x1, Pallas kernels, body(): pl.pallas_call(hand_over, out_shape=tuple((jax.ShapeDtypeStruct(r.shape,...  2.46 us

profile of v7, /device:TPU:0, one launch (start us, length us, event | category | flops | bytes accessed | tf_op | source)
XLA Modules:
  0.0 77.9 jit_solution(14051975333007455231)
XLA Ops:
  0.6 74.8 %encoder_backward.1 = (bf16[8192,128]{1,0:T(8,128)(2,1)}, f32[32,128]{1,0:T(8,128)}, f32[32,128]{1,0:T(8,128)}) custom-call(bf16[8192,128]{1,0:T(8,128)(2,1)} %feat.1, bf16[32,128]{1,0:T(8,128)(2,1)} %w6.1, bf16[32,128]{1,0:T(8,128)(2,1)} %w7.1, bf16[2048,128]{1,0:T(8,128)(2,1)} %grads_in.1, s32[65536]{0:T(1024)} %dest_in.1, s32[4]{0:T(128)} %lens_in.1), custom_call_target="tpu_custom_call" | custom-call | tf_op jit(solution)/shard_map/encoder_backward/pallas_call | solution.py:478
  75.5 2.5 %hand_over.1 = (bf16[8192,128]{1,0:T(8,128)(2,1)}, f32[32,128]{1,0:T(8,128)}, f32[32,128]{1,0:T(8,128)}) custom-call(bf16[8192,128]{1,0:T(8,128)(2,1)} %get-tuple-element.6.gf, f32[32,128]{1,0:T(8,128)} %get-tuple-element.7.g6, f32[32,128]{1,0:T(8,128)} %get-tuple-element.8.g7), custom_call_target="tpu_custom_call" | custom-call | tf_op jit(solution)/shard_map/hand_over/pallas_call | solution.py:534

commit v8 on v6

--- a/solution.py
+++ b/solution.py
@@ -169,14 +169,6 @@
             meta[odd] = dot(digits, pick, ((1,), (1,)))
 
     number_slots()
-    for i in range(1, 4):
-        va(i).wait()
-        ux(i).wait()
-    for i in range(1, 4):
-        vb(i).start()
-        ua(0, i).start()
-        ua(1, i).start()
-
     def routed(k):
         return remote(
             obox.at[k], arrived.at[k], rt_s.at[k], rt_r.at[k],
@@ -211,6 +203,16 @@
         @pl.when(g == 0)
         def _():
             own_block.start()
+
+        @pl.when(i == 0)
+        def _():
+            for n in range(1, 4):
+                va(n).wait()
+                ux(n).wait()
+            for n in range(1, 4):
+                vb(n).start()
+                ua(0, n).start()
+                ua(1, n).start()
 
     for i in range(1, 4):
         vb(i).wait()

time: 77.7 us -> 81.5 us (1.049)
  Pallas kernels: 76.9 us -> 80.6 us
    pallas_call x1, Pallas kernels: 74.4 us -> 78.2 us  [body(): pl.pallas_call(kernel, out_shape=(jax.ShapeDtypeStruct(features.shape, BF...]
where the time goes in v8:
time: 81.5 us; the launch traced here: 81.3 us
  Pallas kernels  80.6 us (99%)
    pallas_call x1, Pallas kernels, body(): pl.pallas_call(kernel, out_shape=(jax.ShapeDtypeStruct(features.shape, BF...  78.2 us
    pallas_call x1, Pallas kernels, body(): pl.pallas_call(hand_over, out_shape=tuple((jax.ShapeDtypeStruct(r.shape,...  2.46 us

profile of v8, /device:TPU:0, one launch (start us, length us, event | category | flops | bytes accessed | tf_op | source)
XLA Modules:
  0.0 81.3 jit_solution(1299579838070923945)
XLA Ops:
  0.6 78.2 %encoder_backward.1 = (bf16[8192,128]{1,0:T(8,128)(2,1)}, f32[32,128]{1,0:T(8,128)}, f32[32,128]{1,0:T(8,128)}) custom-call(bf16[8192,128]{1,0:T(8,128)(2,1)} %feat.1, bf16[32,128]{1,0:T(8,128)(2,1)} %w6.1, bf16[32,128]{1,0:T(8,128)(2,1)} %w7.1, bf16[2048,128]{1,0:T(8,128)(2,1)} %grads_in.1, s32[65536]{0:T(1024)} %dest_in.1, s32[4]{0:T(128)} %lens_in.1), custom_call_target="tpu_custom_call" | custom-call | tf_op jit(solution)/shard_map/encoder_backward/pallas_call | solution.py:471
  78.8 2.5 %hand_over.1 = (bf16[8192,128]{1,0:T(8,128)(2,1)}, f32[32,128]{1,0:T(8,128)}, f32[32,128]{1,0:T(8,128)}) custom-call(bf16[8192,128]{1,0:T(8,128)(2,1)} %get-tuple-element.6.gf, f32[32,128]{1,0:T(8,128)} %get-tuple-element.7.g6, f32[32,128]{1,0:T(8,128)} %get-tuple-element.8.g7), custom_call_target="tpu_custom_call" | custom-call | tf_op jit(solution)/shard_map/hand_over/pallas_call | solution.py:525
